TPU v7x, 32 devices: a whole 2x2x4 slice. The times are simulated.
32 devices in a mesh: batch: 8 (over z, y), chan: 4 (over x, core).
Axes of the slice: x: 2, y: 2, z: 4, core: 2. Of those that a mesh axis runs over, the one named last changes fastest.
Arguments:
- entry_activation: bfloat16 [64, 14, 14, 1024], P('batch', None, None, 'chan'), may hold values from -16 to 16
- image_bounds: int32 [64, 2], P('batch'), may hold values from 8 to 14, as said below
- loss_sensitivity: bfloat16 [64, 7, 7, 2048], P('batch', None, None, 'chan'), may hold values from -6 to 6
- first_contract_kernel: bfloat16 [1024, 512], P(None, 'chan'), may hold values from -0.1875 to 0.1875
- first_strided_kernel: bfloat16 [3, 3, 512, 512], P(None, None, None, 'chan'), may hold values from -0.09375 to 0.09375
- first_enlarge_kernel: bfloat16 [512, 2048], P(None, 'chan'), may hold values from -0.25 to 0.25
- projection_kernel: bfloat16 [1024, 2048], P(None, 'chan'), may hold values from -0.1875 to 0.1875
- second_contract_kernel: bfloat16 [2048, 512], P(None, 'chan'), may hold values from -0.125 to 0.125
- second_spatial_kernel: bfloat16 [3, 3, 512, 512], P(None, None, None, 'chan'), may hold values from -0.09375 to 0.09375
- second_enlarge_kernel: bfloat16 [512, 2048], P(None, 'chan'), may hold values from -0.25 to 0.25
- bottleneck_gains: float32 [4, 512], P(None, 'chan'), may hold values from 0.5 to 1.5
- bottleneck_biases: float32 [4, 512], P(None, 'chan'), may hold values from -2 to 2
- wide_gain_vector: float32 [3, 2048], P(None, 'chan'), may hold values from 0.5 to 1.5
- wide_bias_vector: float32 [3, 2048], P(None, 'chan'), may hold values from -2 to 2
Outputs:
- result: bfloat16 [64, 7, 7, 2048], P('batch', None, None, 'chan')
- inputs_grad: bfloat16 [64, 14, 14, 1024], P('batch', None, None, 'chan')
- reducing_grad: float32 [1024, 512], P(None, 'chan')
- spatial_grad: float32 [3, 3, 512, 512], P(None, None, None, 'chan')
- widening_grad: float32 [512, 2048], P(None, 'chan')
- shortcut_grad: float32 [1024, 2048], P(None, 'chan')
- narrowing_grad: float32 [2048, 512], P(None, 'chan')
- middle_grad: float32 [3, 3, 512, 512], P(None, None, None, 'chan')
- expanding_grad: float32 [512, 2048], P(None, 'chan')
- scale_gradient: float32 [4, 512], P(None, 'chan')
- offset_gradient: float32 [4, 512], P(None, 'chan')
- amplitude_gradient: float32 [3, 2048], P(None, 'chan')
- baseline_gradient: float32 [3, 2048], P(None, 'chan')
Inputs may be any that keep to these rules, and one draw needn't show every extreme that they name: `image_bounds`: each image's valid region is the top-left corner of the padded 14 x 14 grid; rows and columns are even.
All inputs are finite; a program needn't handle non-finite values.
Results may differ from a plain program's by a relative error of at most 0.025.
Values may be sent and summed in bfloat16 or wider, within the bound.
No kernel may reach another device: no remote copies, remote signals or barrier semaphores. Data moves between devices by JAX's collectives and lax.ppermute only.
A program may use at most 128 MiB of HBM per device.

v0:
```python
import functools

import jax
import jax.numpy as jnp
from jax import lax
from jax.experimental import pallas as pl
from jax.experimental.pallas import tpu as pltpu
from jax.sharding import PartitionSpec as P

EPS = 1e-05
BF = jnp.bfloat16
F32 = jnp.float32
GELU_A = 0.7978845608028654
GELU_B = 0.044715
LANES = 128
IMAGES = 8
CELLS = 8
CHUNK = CELLS * IMAGES
VMEM_LIMIT = 56 * 1024 * 1024


def dot(a, b, dims=((1,), (0,))):
    return lax.dot_general(a, b, (dims, ((), ())), preferred_element_type=F32)


def gelu(v):
    return 0.5 * v * (1.0 + jnp.tanh(GELU_A * v * (1.0 + GELU_B * v * v)))


def gelu_slope(v):
    square = v * v
    t = jnp.tanh(GELU_A * v * (1.0 + GELU_B * square))
    return 0.5 * (1.0 + t) * (1.0 + v * (1.0 - t) * (GELU_A + 3.0 * GELU_A * GELU_B * square))


class Masks:
    def __init__(self, bounds):
        image = lax.broadcasted_iota(jnp.int32, (IMAGES, LANES), 0)
        high = jnp.zeros((IMAGES, LANES), jnp.int32)
        low = jnp.zeros((IMAGES, LANES), jnp.int32)
        inside = jnp.int32(0)
        outside = jnp.int32(0)
        for n in range(IMAGES):
            h, w = bounds[n, 0], bounds[n, 1]
            high = jnp.where(image == n, h, high)
            low = jnp.where(image == n, w, low)
            inside = inside + h * w
            outside = outside + lax.shift_right_logical(h + 1, 1) * lax.shift_right_logical(w + 1, 1)
        self.high = high[None]
        self.low = low[None]
        self.column = lax.broadcasted_iota(jnp.int32, (CELLS, IMAGES, LANES), 0) * 2
        self.local_in = inside.astype(F32)
        self.local_out = outside.astype(F32)

    def large(self, row, parity):
        return (row < self.high) & (self.column + parity < self.low)

    def small(self, row):
        return (2 * row < self.high) & (self.column < self.low)


def keep(mask, value):
    return jnp.where(mask, value, 0.0)


def cube(rows):
    return rows.astype(F32).reshape(CELLS, IMAGES, LANES)


def flat(value):
    return value.reshape(CHUNK, LANES)


def total_of(value):
    return jnp.sum(value, axis=0)


def row_sum(value):
    return jnp.sum(value, axis=0, keepdims=True)


def at(step, size):
    return pl.ds(pl.multiple_of(step * size, size), size)


def lane_block(index, width=LANES):
    return pl.ds(pl.multiple_of(index * width, width), width)


def push_left(value):
    return jnp.concatenate([value[1:], jnp.zeros((1, IMAGES, LANES), F32)], axis=0)


def push_right(value):
    return jnp.concatenate([jnp.zeros((1, IMAGES, LANES), F32), value[:-1]], axis=0)


def norm_of(got, who, batch, chan, k, row, local, count):
    column = who[0] ^ k
    total = got[column]
    for n in range(1, batch):
        total = total + got[n * chan + column]
    mine = got[who[1] * chan + column]
    mean = total[row : row + 1] / count
    inverse = lax.rsqrt(total[row + 1 : row + 2] / count - mean * mean + EPS)
    return mine[row : row + 1] / local - mean, inverse


def whole(got):
    total = got[0]
    for n in range(1, got.shape[0]):
        total = total + got[n]
    return total


def in_vmem(kernel, ins, outs, scratch=(), flops=0, name=None):
    specs = [
        pl.BlockSpec(memory_space=pltpu.SMEM if v.dtype == jnp.int32 else pltpu.VMEM) for v in ins
    ]
    size = sum(v.size * v.dtype.itemsize for v in ins)
    return pl.pallas_call(
        kernel,
        out_shape=[jax.ShapeDtypeStruct(s, d) for s, d in outs],
        in_specs=specs,
        out_specs=[pl.BlockSpec(memory_space=pltpu.VMEM) for _ in outs],
        scratch_shapes=[pltpu.VMEM(s, d) for s, d in scratch],
        compiler_params=pltpu.CompilerParams(vmem_limit_bytes=VMEM_LIMIT),
        cost_estimate=pl.CostEstimate(flops=flops, bytes_accessed=size, transcendentals=0),
        name=name,
    )(*ins)


def sums_of(z, chunks, lanes, mask=None):
    def step(t, carry):
        value = cube(z[at(t, CHUNK), lanes])
        if mask is not None:
            value = keep(mask(t), value)
        return carry[0] + total_of(value), carry[1] + total_of(value * value)

    zero = jnp.zeros((IMAGES, LANES), F32)
    total, squares = lax.fori_loop(0, chunks, step, (zero, zero))
    return row_sum(total), row_sum(squares)


def centre_into(out, z, chunks, lanes, mean):
    def step(t, _):
        out[at(t, CHUNK), lanes] = (z[at(t, CHUNK), lanes] - mean).astype(BF)
        return 0

    lax.fori_loop(0, chunks, step, 0)


def broadcast_rows(out, rows):
    block = jnp.concatenate(
        list(rows) + [jnp.zeros((out.shape[1] - len(rows), LANES), F32)]
        if len(rows) < out.shape[1]
        else list(rows),
        axis=0,
    )
    out[...] = jnp.broadcast_to(block[None], out.shape)


def fill_rows(out, rows):
    for n, row in enumerate(rows):
        out[n : n + 1, :] = row
    if len(rows) < out.shape[0]:
        out[len(rows) :, :] = jnp.zeros((out.shape[0] - len(rows), LANES), F32)


def permutation(side, back):
    size = 16 * IMAGES if side else 8 * IMAGES
    one = lax.broadcasted_iota(jnp.int32, (size, size), 1 if back else 0)
    other = lax.broadcasted_iota(jnp.int32, (size, size), 0 if back else 1)
    image = one & 7
    column = (one >> 3) & 7
    if side:
        target = image * 16 + column * 2 + (one >> 6)
    else:
        target = image * 8 + column
    return (other == target).astype(F32).astype(BF)


def enter_kernel(bounds, x, out, held):
    masks = Masks(bounds)
    order = permutation(True, False)
    held[...] = jnp.zeros(held.shape, BF)
    width = x.shape[3]

    def step(r, _):
        for n in range(IMAGES):
            held[16 * n : 16 * n + x.shape[2], :] = x[n, r]
        moved = dot(order, held[...])
        for parity in range(2):
            mask = masks.large(r, parity)
            for q in range(width // LANES):
                part = moved[parity * CHUNK : (parity + 1) * CHUNK, q * LANES : (q + 1) * LANES]
                out[at(r * 2 + parity, CHUNK), q * LANES : (q + 1) * LANES] = flat(
                    keep(mask, cube(part))
                ).astype(BF)
        return 0

    lax.fori_loop(0, x.shape[1], step, 0)


def loss_kernel(x, out, held):
    order = permutation(False, False)
    held[...] = jnp.zeros(held.shape, F32)

    def step(i, _):
        for n in range(IMAGES):
            held[8 * n : 8 * n + x.shape[2], :] = x[n, i].astype(F32)
        out[at(i, CHUNK), :] = dot(order, held[...].astype(BF)).astype(BF)
        return 0

    lax.fori_loop(0, x.shape[1], step, 0)


def first_kernel(chan, bounds, who, *refs):
    source, (w, zc, stats, z) = refs[:chan], refs[chan:]
    masks = Masks(bounds)
    rows, depth = source[0].shape
    part = rows // 4

    def step(t, _):
        total = None
        for k in range(chan):
            term = dot(source[k][at(t, part), :], w[at(who[0] ^ k, depth), :])
            total = term if total is None else total + term
        z[at(t, part), :] = total
        return 0

    lax.fori_loop(0, 4, step, 0)
    chunks = rows // CHUNK
    total, squares = sums_of(z, chunks, slice(0, LANES))
    ones = jnp.ones((1, LANES), F32)
    broadcast_rows(stats, (total, squares, ones * masks.local_in, ones * masks.local_out))
    centre_into(zc, z, chunks, slice(0, LANES), total / masks.local_in)


def shortcut_kernel(chan, bounds, who, *refs):
    source, (w, even, zc, stats, z) = refs[:chan], refs[chan:]
    masks = Masks(bounds)
    rows, width = z.shape
    depth = source[0].shape[1]
    chunks = rows // CHUNK
    for k in range(chan):
        for t in range(chunks):
            even[t * CHUNK : (t + 1) * CHUNK, lane_block(who[0] ^ k, depth)] = source[k][
                4 * t * CHUNK : (4 * t + 1) * CHUNK, :
            ]
    z[...] = dot(even[...], w[...])
    blocks = width // LANES
    for q in range(blocks):
        lanes = slice(q * LANES, (q + 1) * LANES)
        total, squares = sums_of(z, chunks, lanes)
        stats[q : q + 1, :] = total
        stats[blocks + q : blocks + q + 1, :] = squares
        centre_into(zc, z, chunks, lanes, total / masks.local_out)


def strided_kernel(batch, chan, bounds, who, got, *refs):
    near, (tabs, w, extra, a, zc, stats, norms, counts, z) = refs[:chan], refs[chan:]
    masks = Masks(bounds)
    total = whole(got)
    count_in, count_out = total[2:3] / chan, total[3:4] / chan
    fill_rows(counts, (count_in, count_out))
    params = []
    for k in range(chan):
        norm = norm_of(got, who, batch, chan, k, 0, masks.local_in, count_in)
        params.append(norm)
        norms[2 * k : 2 * k + 1, :] = norm[0]
        norms[2 * k + 1 : 2 * k + 2, :] = norm[1]
    width = a.shape[3]
    for tap in range(3):
        a[tap, 0, 0:CHUNK, :] = jnp.zeros((CHUNK, width), BF)
    side = near[0].shape[0] // (2 * CHUNK)

    def step(r, _):
        line = r + 1
        half, place = line & 1, lax.shift_right_logical(line, 1)
        for k in range(chan):
            lanes = lane_block(who[0] ^ k)
            scale = params[k][1] * tabs[k, 0:1, :]
            shift = params[k][0] * scale + tabs[k, 4:5, :]
            for parity in range(2):
                pre = cube(near[k][at(r * 2 + parity, CHUNK), :]) * scale + shift
                value = keep(masks.large(r, parity), gelu(pre))
                a[1 + parity, half, at(place, CHUNK), lanes] = flat(value).astype(BF)
                if parity:
                    a[0, half, at(place, CHUNK), lanes] = flat(push_right(value)).astype(BF)
        return 0

    lax.fori_loop(0, side, step, 0)
    rows = z.shape[0]
    acc = None
    for i, (half, first) in enumerate(((0, 0), (1, 0), (0, CHUNK))):
        for j in range(3):
            term = dot(a[j, half, first : first + rows, :], w[i, j])
            acc = term if acc is None else acc + term
    z[...] = acc
    chunks = rows // CHUNK
    total, squares = sums_of(z, chunks, slice(0, LANES), masks.small)
    block = jnp.concatenate([total, squares, jnp.zeros((6, LANES), F32), extra[...]], axis=0)
    stats[...] = jnp.broadcast_to(block[None], stats.shape)
    centre_into(zc, z, chunks, slice(0, LANES), total / masks.local_out)


def activate_into(near, params, tabs, gain, chan, who, masks, chunks, store):
    def step(t, _):
        mask = masks.small(t)
        for k in range(chan):
            scale = params[k][1] * tabs[k, gain : gain + 1, :]
            shift = params[k][0] * scale + tabs[k, gain + 4 : gain + 5, :]
            value = keep(mask, gelu(cube(near[k][at(t, CHUNK), :]) * scale + shift))
            store(t, lane_block(who[0] ^ k), value)
        return 0

    lax.fori_loop(0, chunks, step, 0)


def store_norms(norms, params):
    for k, norm in enumerate(params):
        norms[2 * k : 2 * k + 1, :] = norm[0]
        norms[2 * k + 1 : 2 * k + 2, :] = norm[1]


def enlarge_kernel(batch, chan, bounds, who, got, *refs):
    near, (tabs, counts, w, a, zc, stats, norms, z) = refs[:chan], refs[chan:]
    masks = Masks(bounds)
    count = counts[1:2, :]
    params = [norm_of(got, who, batch, chan, k, 0, masks.local_out, count) for k in range(chan)]
    store_norms(norms, params)
    chunks = z.shape[0] // CHUNK

    def store(t, lanes, value):
        a[at(t, CHUNK), lanes] = flat(value).astype(BF)

    activate_into(near, params, tabs, 1, chan, who, masks, chunks, store)
    z[...] = dot(a[...], w[...])
    rows = wide_sums(z, zc, chunks, masks)
    broadcast_rows(stats, rows)


def wide_sums(z, zc, chunks, masks):
    blocks = z.shape[1] // LANES
    totals, squares = [], []
    for q in range(blocks):
        lanes = slice(q * LANES, (q + 1) * LANES)
        total, square = sums_of(z, chunks, lanes)
        totals.append(total)
        squares.append(square)
        if zc is not None:
            centre_into(zc, z, chunks, lanes, total / masks.local_out)
    return totals + squares


def wide_norm(got, who, batch, chan, k, row, blocks, local, count):
    column = who[0] ^ k
    total = got[column]
    for n in range(1, batch):
        total = total + got[n * chan + column]
    mine = got[who[1] * chan + column]
    mean = total[row : row + blocks] / count
    inverse = lax.rsqrt(total[row + blocks : row + 2 * blocks] / count - mean * mean + EPS)
    return mine[row : row + blocks] / local - mean, inverse


def merge_kernel(batch, chan, bounds, who, got3, got2, *refs):
    near3, nears = refs[:chan], refs[chan : 2 * chan]
    tabs, counts, w, y, own, zc, stats, norms, z = refs[2 * chan :]
    masks = Masks(bounds)
    count = counts[1:2, :]
    rows, width = near3[0].shape
    blocks = width // LANES
    chunks = rows // CHUNK
    lines = []
    for k in range(chan):
        one = wide_norm(got3, who, batch, chan, k, 0, blocks, masks.local_out, count)
        two = wide_norm(got2, who, batch, chan, k, 8, blocks, masks.local_out, count)
        if k == 0:
            for n, value in enumerate(one + two):
                norms[n * blocks : (n + 1) * blocks, :] = value
        gain, bias = 8, 8 + 3 * blocks
        scale3 = one[1] * tabs[k, gain : gain + blocks, :]
        scales = two[1] * tabs[k, gain + blocks : gain + 2 * blocks, :]
        shift = (
            one[0] * scale3
            + two[0] * scales
            + tabs[k, bias : bias + blocks, :]
            + tabs[k, bias + blocks : bias + 2 * blocks, :]
        )
        lines.append((scale3, scales, shift))

    def step(t, _):
        mask = masks.small(t)
        for k in range(chan):
            scale3, scales, shift = lines[k]
            for q in range(blocks):
                lanes = slice(q * LANES, (q + 1) * LANES)
                pre = (
                    cube(near3[k][at(t, CHUNK), lanes]) * scale3[q : q + 1]
                    + cube(nears[k][at(t, CHUNK), lanes]) * scales[q : q + 1]
                    + shift[q : q + 1]
                )
                value = flat(keep(mask, gelu(pre)))
                if k == 0:
                    own[at(t, CHUNK), lanes] = value
                y[at(t, CHUNK), lane_block((who[0] ^ k) * blocks + q)] = value.astype(BF)
        return 0

    lax.fori_loop(0, chunks, step, 0)
    z[...] = dot(y[...], w[...])
    total, squares = sums_of(z, chunks, slice(0, LANES))
    broadcast_rows(stats, (total, squares))
    centre_into(zc, z, chunks, slice(0, LANES), total / masks.local_out)


def spatial_kernel(batch, chan, bounds, who, got, *refs):
    near, (tabs, counts, w, a, zc, stats, norms, held, z) = refs[:chan], refs[chan:]
    masks = Masks(bounds)
    count = counts[1:2, :]
    params = [norm_of(got, who, batch, chan, k, 0, masks.local_out, count) for k in range(chan)]
    store_norms(norms, params)
    rows, width = a.shape
    chunks = rows // CHUNK
    for tap in range(3):
        held[tap, 0:CHUNK, :] = jnp.zeros((CHUNK, width), BF)
        held[tap, rows + CHUNK : rows + 2 * CHUNK, :] = jnp.zeros((CHUNK, width), BF)

    def store(t, lanes, value):
        plain = flat(value).astype(BF)
        a[at(t, CHUNK), lanes] = plain
        held[1, at(t + 1, CHUNK), lanes] = plain
        held[0, at(t + 1, CHUNK), lanes] = flat(push_right(value)).astype(BF)
        held[2, at(t + 1, CHUNK), lanes] = flat(push_left(value)).astype(BF)

    activate_into(near, params, tabs, 2, chan, who, masks, chunks, store)
    acc = None
    for i in range(3):
        for j in range(3):
            term = dot(held[j, i * CHUNK : i * CHUNK + rows, :], w[i, j])
            acc = term if acc is None else acc + term
    z[...] = acc
    total, squares = sums_of(z, chunks, slice(0, LANES), masks.small)
    broadcast_rows(stats, (total, squares))
    centre_into(zc, z, chunks, slice(0, LANES), total / masks.local_out)


def last_kernel(batch, chan, bounds, who, got, *refs):
    near, (tabs, counts, w, a, z, stats, norms) = refs[:chan], refs[chan:]
    masks = Masks(bounds)
    count = counts[1:2, :]
    params = [norm_of(got, who, batch, chan, k, 0, masks.local_out, count) for k in range(chan)]
    store_norms(norms, params)
    chunks = a.shape[0] // CHUNK

    def store(t, lanes, value):
        a[at(t, CHUNK), lanes] = flat(value).astype(BF)

    activate_into(near, params, tabs, 3, chan, who, masks, chunks, store)
    z[...] = dot(a[...], w[...])
    broadcast_rows(stats, wide_sums(z, None, chunks, masks))


def output_kernel(bounds, got, z, own, loss, tabs, counts, result, g, stats, norms):
    masks = Masks(bounds)
    count = counts[1:2, :]
    total = whole(got)
    rows, width = z.shape
    blocks = width // LANES
    chunks = rows // CHUNK
    mean = total[0:blocks] / count
    inverse = lax.rsqrt(total[blocks : 2 * blocks] / count - mean * mean + EPS)
    norms[0:blocks, :] = mean
    norms[blocks : 2 * blocks, :] = inverse
    gain = tabs[0, 8 + 2 * blocks : 8 + 3 * blocks, :]
    bias = tabs[0, 8 + 5 * blocks : 8 + 6 * blocks, :]
    order = permutation(False, True)
    small = result.shape[2]

    def step(t, carry):
        mask = masks.small(t)
        sums = []
        pieces = []
        for q in range(blocks):
            lanes = slice(q * LANES, (q + 1) * LANES)
            zhat = (cube(z[at(t, CHUNK), lanes]) - mean[q : q + 1]) * inverse[q : q + 1]
            pre = zhat * gain[q : q + 1] + bias[q : q + 1] + cube(own[at(t, CHUNK), lanes])
            pieces.append(flat(keep(mask, gelu(pre))).astype(BF))
            u = keep(mask, gelu_slope(pre)) * cube(loss[at(t, CHUNK), lanes])
            g[at(t, CHUNK), lanes] = flat(u)
            sums.append((carry[q][0] + total_of(u * zhat), carry[q][1] + total_of(u)))
        moved = dot(order, jnp.concatenate(pieces, axis=1))
        for n in range(IMAGES):
            result[n, t] = moved[n * 8 : n * 8 + small, :].astype(BF)
        return tuple(sums)

    zero = jnp.zeros((IMAGES, LANES), F32)
    sums = lax.fori_loop(0, chunks, step, ((zero, zero),) * blocks)
    broadcast_rows(stats, [row_sum(s[0]) for s in sums] + [row_sum(s[1]) for s in sums])


def share_stage(da, near, norms, tabs, gain, chan, batch, who, masks, chunks, pieces, stats):
    zero = jnp.zeros((IMAGES, LANES), F32)
    for k in range(chan):
        lanes = lane_block(who[0] ^ k)
        offset, inverse = norms[2 * k : 2 * k + 1, :], norms[2 * k + 1 : 2 * k + 2, :]
        scale, bias = tabs[k, gain : gain + 1, :], tabs[k, gain + 4 : gain + 5, :]

        def step(t, carry, k=k, lanes=lanes, offset=offset, inverse=inverse, scale=scale, bias=bias):
            share = da[at(t, CHUNK), lanes]
            zhat = (cube(near[k][at(t, CHUNK), :]) + offset) * inverse
            u = keep(masks.small(t), gelu_slope(zhat * scale + bias)) * cube(share)
            pieces[k][at(t, CHUNK), :] = share.astype(pieces[k].dtype)
            return carry[0] + total_of(u * zhat), carry[1] + total_of(u)

        first, second = lax.fori_loop(0, chunks, step, (zero, zero))
        block = jnp.concatenate(
            [row_sum(first), row_sum(second), jnp.zeros((stats.shape[1] - 2, LANES), F32)], axis=0
        )
        for n in range(batch):
            stats[n * chan + (who[0] ^ k)] = block


def own_stage(got, parts, near, norms, tabs, gain, count, masks, chunks, sums, store):
    total = whole(got)
    gg, gb = total[0:1], total[1:2]
    fill_rows(sums, (gg, gb))
    offset, inverse = norms[0:1, :], norms[1:2, :]
    scale, bias = tabs[0, gain : gain + 1, :], tabs[0, gain + 4 : gain + 5, :]
    per_cell, per_hat = gb / count, gg / count
    front = scale * inverse

    def step(t, _):
        mask = masks.small(t)
        da = cube(parts[0][at(t, CHUNK), :])
        for part in parts[1:]:
            da = da + cube(part[at(t, CHUNK), :])
        zhat = (cube(near[at(t, CHUNK), :]) + offset) * inverse
        u = gelu_slope(zhat * scale + bias) * da
        store(t, keep(mask, front * (u - (per_cell + zhat * per_hat))))
        return 0

    lax.fori_loop(0, chunks, step, 0)


def back_last_kernel(batch, chan, bounds, who, got, g, z, norms6, tabs, counts, w, *refs):
    near, (norms, dz, *pieces, stats, sums, da) = refs[:chan], refs[chan:]
    masks = Masks(bounds)
    count = counts[1:2, :]
    total = whole(got)
    rows, width = z.shape
    blocks = width // LANES
    chunks = rows // CHUNK
    gg, gb = total[0:blocks] / count, total[blocks : 2 * blocks] / count
    sums[...] = total
    mean, inverse = norms6[0:blocks, :], norms6[blocks : 2 * blocks, :]
    front = tabs[0, 8 + 2 * blocks : 8 + 3 * blocks, :] * inverse

    def step(t, _):
        mask = masks.small(t)
        for q in range(blocks):
            lanes = slice(q * LANES, (q + 1) * LANES)
            zhat = (cube(z[at(t, CHUNK), lanes]) - mean[q : q + 1]) * inverse[q : q + 1]
            value = cube(g[at(t, CHUNK), lanes]) - (gb[q : q + 1] + zhat * gg[q : q + 1])
            dz[at(t, CHUNK), lanes] = flat(keep(mask, front[q : q + 1] * value)).astype(BF)
        return 0

    lax.fori_loop(0, chunks, step, 0)
    da[...] = dot(dz[...], w[...], ((1,), (1,)))
    share_stage(da, near, norms, tabs, 3, chan, batch, who, masks, chunks, pieces, stats)


def back_spatial_kernel(batch, chan, bounds, who, got, *refs):
    parts, refs = refs[:chan], refs[chan:]
    own, norms5, tabs, counts, w = refs[:5]
    near, (norms, spread, *pieces, stats, sums, held, da) = refs[5 : 5 + chan], refs[5 + chan :]
    masks = Masks(bounds)
    rows = own.shape[0]
    chunks = rows // CHUNK
    for tap in range(3):
        held[tap, 0:CHUNK, :] = jnp.zeros((CHUNK, LANES), BF)
        held[tap, rows + CHUNK : rows + 2 * CHUNK, :] = jnp.zeros((CHUNK, LANES), BF)

    def store(t, value):
        held[1, at(t + 1, CHUNK), :] = flat(value).astype(BF)
        held[0, at(t + 1, CHUNK), :] = flat(push_left(value)).astype(BF)
        held[2, at(t + 1, CHUNK), :] = flat(push_right(value)).astype(BF)

    own_stage(got, parts, own, norms5, tabs, 3, counts[1:2, :], masks, chunks, sums, store)
    acc = None
    for i in range(3):
        for j in range(3):
            value = held[j, (2 - i) * CHUNK : (2 - i) * CHUNK + rows, :]
            spread[:, (3 * i + j) * LANES : (3 * i + j + 1) * LANES] = value
            term = dot(value, w[i, j], ((1,), (1,)))
            acc = term if acc is None else acc + term
    da[...] = acc
    share_stage(da, near, norms, tabs, 2, chan, batch, who, masks, chunks, pieces, stats)


def back_contract_kernel(bounds, got, *refs):
    *parts, own, norms, tabs, counts, dz, sums = refs
    masks = Masks(bounds)

    def store(t, value):
        dz[at(t, CHUNK), :] = flat(value).astype(BF)

    own_stage(got, parts, own, norms, tabs, 2, counts[1:2, :], masks, own.shape[0] // CHUNK, sums, store)


def back_merge_kernel(chan, bounds, *refs):
    dz, w = refs[:chan], refs[chan : 2 * chan]
    g, near3, nears, norms, tabs, g1, stats, dy = refs[2 * chan :]
    masks = Masks(bounds)
    rows, width = g.shape
    blocks = width // LANES
    chunks = rows // CHUNK
    acc = None
    for k in range(chan):
        term = dot(dz[k][...], w[k][...], ((1,), (1,)))
        acc = term if acc is None else acc + term
    dy[...] = acc
    zero = jnp.zeros((IMAGES, LANES), F32)
    lines = [[], [], []]
    for q in range(blocks):
        lanes = slice(q * LANES, (q + 1) * LANES)
        off3, inv3, offs, invs = (norms[n * blocks + q : n * blocks + q + 1, :] for n in range(4))
        gain, bias = 8, 8 + 3 * blocks
        gain3, gains = tabs[0, gain + q : gain + q + 1, :], tabs[0, gain + blocks + q : gain + blocks + q + 1, :]
        shift = tabs[0, bias + q : bias + q + 1, :] + tabs[0, bias + blocks + q : bias + blocks + q + 1, :]

        def step(t, carry):
            zhat3 = (cube(near3[at(t, CHUNK), lanes]) + off3) * inv3
            zhats = (cube(nears[at(t, CHUNK), lanes]) + offs) * invs
            pre = zhat3 * gain3 + zhats * gains + shift
            up = cube(g[at(t, CHUNK), lanes]) + cube(dy[at(t, CHUNK), lanes])
            u = keep(masks.small(t), gelu_slope(pre)) * up
            g1[at(t, CHUNK), lanes] = flat(u)
            return (
                carry[0] + total_of(u * zhat3),
                carry[1] + total_of(u * zhats),
                carry[2] + total_of(u),
            )

        done = lax.fori_loop(0, chunks, step, (zero, zero, zero))
        for n in range(3):
            lines[n].append(row_sum(done[n]))
    broadcast_rows(stats, lines[0] + lines[1] + lines[2])


def back_enlarge_kernel(batch, chan, bounds, who, got, g1, near3, nears, norms3, tabs, counts, w, *refs):
    near, (norms, dz3, dzs, *pieces, stats, sums, da) = refs[:chan], refs[chan:]
    masks = Masks(bounds)
    count = counts[1:2, :]
    total = whole(got)
    sums[...] = total
    rows, width = g1.shape
    blocks = width // LANES
    chunks = rows // CHUNK
    total = total / count
    gg3, ggs, gb = (total[n * blocks : (n + 1) * blocks] for n in range(3))
    off3, inv3, offs, invs = (norms3[n * blocks : (n + 1) * blocks, :] for n in range(4))
    front3 = tabs[0, 8 : 8 + blocks, :] * inv3
    fronts = tabs[0, 8 + blocks : 8 + 2 * blocks, :] * invs

    def step(t, _):
        mask = masks.small(t)
        for q in range(blocks):
            lanes = slice(q * LANES, (q + 1) * LANES)
            line = slice(q, q + 1)
            u = cube(g1[at(t, CHUNK), lanes]) - gb[line]
            zhat3 = (cube(near3[at(t, CHUNK), lanes]) + off3[line]) * inv3[line]
            zhats = (cube(nears[at(t, CHUNK), lanes]) + offs[line]) * invs[line]
            dz3[at(t, CHUNK), lanes] = flat(keep(mask, front3[line] * (u - zhat3 * gg3[line]))).astype(BF)
            dzs[at(t, CHUNK), lanes] = flat(keep(mask, fronts[line] * (u - zhats * ggs[line]))).astype(BF)
        return 0

    lax.fori_loop(0, chunks, step, 0)
    da[...] = dot(dz3[...], w[...], ((1,), (1,)))
    share_stage(da, near, norms, tabs, 1, chan, batch, who, masks, chunks, pieces, stats)


def back_strided_kernel(bounds, got, *refs):
    *parts, own, norms, tabs, counts, dz, moved, sums, held = refs
    masks = Masks(bounds)
    rows = own.shape[0]
    for tap in range(2):
        held[tap, rows : rows + CHUNK, :] = jnp.zeros((CHUNK, LANES), BF)

    def store(t, value):
        plain = flat(value).astype(BF)
        dz[at(t, CHUNK), :] = plain
        held[0, at(t, CHUNK), :] = plain
        held[1, at(t, CHUNK), :] = flat(push_left(value)).astype(BF)

    own_stage(got, parts, own, norms, tabs, 1, counts[1:2, :], masks, rows // CHUNK, sums, store)
    for down in range(2):
        for right in range(2):
            n = 2 * down + right
            moved[:, n * LANES : (n + 1) * LANES] = held[right, down * CHUNK : down * CHUNK + rows, :]


TAPS = {0: ((1, 0),), 1: ((2, 0), (0, 1))}


def back_first_kernel(chan, bounds, *refs):
    dz, (w, near, norms, tabs, u_out, stats, held, da) = refs[:chan], refs[chan:]
    masks = Masks(bounds)
    rows = dz[0].shape[0]
    chunks = rows // CHUNK
    for tap in range(2):
        held[tap, rows : rows + CHUNK, :] = jnp.zeros((CHUNK, chan * LANES), BF)

    def shift(t, _):
        for k in range(chan):
            lanes = slice(k * LANES, (k + 1) * LANES)
            value = dz[k][at(t, CHUNK), :]
            held[0, at(t, CHUNK), lanes] = value
            held[1, at(t, CHUNK), lanes] = flat(push_left(cube(value))).astype(BF)
        return 0

    lax.fori_loop(0, chunks, shift, 0)
    offset, inverse = norms[0:1, :], norms[1:2, :]
    scale, bias = tabs[0, 0:1, :], tabs[0, 4:5, :]
    zero = jnp.zeros((IMAGES, LANES), F32)
    sums = (zero, zero)
    for p in range(2):
        for q in range(2):
            acc = None
            for a, down in TAPS[p]:
                for b, right in TAPS[q]:
                    term = dot(held[right, down * CHUNK : down * CHUNK + rows, :], w[a, b], ((1,), (1,)))
                    acc = term if acc is None else acc + term
            da[...] = acc

            def step(t, carry, p=p, q=q):
                r = 2 * t + p
                place = at(r * 2 + q, CHUNK)
                zhat = (cube(near[place, :]) + offset) * inverse
                u = keep(masks.large(r, q), gelu_slope(zhat * scale + bias)) * cube(da[at(t, CHUNK), :])
                u_out[place, :] = flat(u)
                return carry[0] + total_of(u * zhat), carry[1] + total_of(u)

            sums = lax.fori_loop(0, chunks, step, sums)
    broadcast_rows(stats, (row_sum(sums[0]), row_sum(sums[1])))


def back_first_own_kernel(bounds, got, u, near, norms, tabs, counts, dz, sums):
    masks = Masks(bounds)
    count = counts[0:1, :]
    total = whole(got)
    gg, gb = total[0:1], total[1:2]
    fill_rows(sums, (gg, gb))
    per_cell, per_hat = gb / count, gg / count
    offset, inverse = norms[0:1, :], norms[1:2, :]
    front = tabs[0, 0:1, :] * inverse

    def step(r, _):
        for parity in range(2):
            place = at(r * 2 + parity, CHUNK)
            zhat = (cube(near[place, :]) + offset) * inverse
            value = front * (cube(u[place, :]) - (per_cell + zhat * per_hat))
            dz[place, :] = flat(keep(masks.large(r, parity), value)).astype(BF)
        return 0

    lax.fori_loop(0, u.shape[0] // (2 * CHUNK), step, 0)


def leave_kernel(chan, bounds, *refs):
    dz, dzs = refs[:chan], refs[chan : 2 * chan]
    w, ws, out, dm, extra = refs[2 * chan :]
    masks = Masks(bounds)
    order = permutation(True, True)
    wide = dzs[0].shape[1]
    acc = None
    for k in range(chan):
        term = dot(dzs[k][...], ws[:, k * wide : (k + 1) * wide], ((1,), (1,)))
        acc = term if acc is None else acc + term
    extra[...] = acc
    side, width = out.shape[1], out.shape[3]
    part = dm.shape[0] // 4

    def product(t, _):
        total = None
        for k in range(chan):
            term = dot(dz[k][at(t, part), :], w[:, k * LANES : (k + 1) * LANES], ((1,), (1,)))
            total = term if total is None else total + term
        dm[at(t, part), :] = total
        return 0

    lax.fori_loop(0, 4, product, 0)

    def step(i, _):
        for p in range(2):
            r = 2 * i + p
            line = []
            for parity in range(2):
                mask = masks.large(r, parity)
                blocks = []
                for q in range(width // LANES):
                    lanes = slice(q * LANES, (q + 1) * LANES)
                    value = cube(dm[at(r * 2 + parity, CHUNK), lanes])
                    if p == 0 and parity == 0:
                        value = value + cube(extra[at(i, CHUNK), lanes])
                    blocks.append(flat(keep(mask, value)).astype(BF))
                line.append(jnp.concatenate(blocks, axis=1))
            moved = dot(order, jnp.concatenate(line, axis=0))
            for n in range(IMAGES):
                out[n, r] = moved[n * 16 : n * 16 + out.shape[2], :].astype(BF)
        return 0

    lax.fori_loop(0, side // 2, step, 0)


def solution(mesh):
    batch = mesh.shape["batch"]
    chan = mesh.shape["chan"]
    everyone = ("batch", "chan")
    devices = batch * chan

    def swap(v, mask, axis="chan"):
        return lax.ppermute(v, axis, [(k, k ^ mask) for k in range(mesh.shape[axis])])

    def gather(v):
        found = {0: v}
        mask = chan // 2
        while mask:
            for k in list(found):
                found[k ^ mask] = swap(found[k], mask)
            mask //= 2
        return [found[k] for k in range(chan)]

    def gather_direct(v):
        return [v] + [swap(v, k) for k in range(1, chan)]

    def deliver(pieces):
        return [pieces[0]] + [swap(pieces[k], k) for k in range(1, chan)]

    def exchange(stats):
        return lax.all_to_all(stats, everyone, 0, 0)

    def exchange_batch(stats):
        return lax.all_to_all(stats, "batch", 0, 0)

    def local(
        entry_activation,
        image_bounds,
        loss_sensitivity,
        first_contract_kernel,
        first_strided_kernel,
        first_enlarge_kernel,
        projection_kernel,
        second_contract_kernel,
        second_spatial_kernel,
        second_enlarge_kernel,
        bottleneck_gains,
        bottleneck_biases,
        wide_gain_vector,
        wide_bias_vector,
    ):
        images, side, _, quarter = entry_activation.shape
        small = side // 2
        me = lax.axis_index("chan")
        who = jnp.stack([me, lax.axis_index("batch")]).astype(jnp.int32)
        wide = first_enlarge_kernel.shape[1]
        blocks = wide // LANES
        rows, large = small * CHUNK, side * 2 * CHUNK
        depth = quarter * chan
        mid = first_contract_kernel.shape[1] * chan
        bounds = image_bounds
        piece = ((rows, LANES), BF)

        table = jnp.concatenate(
            [
                bottleneck_gains,
                bottleneck_biases,
                wide_gain_vector.reshape(-1, LANES),
                wide_bias_vector.reshape(-1, LANES),
            ]
        )
        tabs = jnp.stack(gather_direct(table))

        def received_rows(v, axis=0):
            size = v.shape[axis] // chan
            cut = [lax.dynamic_slice_in_dim(v, (me ^ k) * size, size, axis) for k in range(chan)]
            return deliver(cut)

        w4t = received_rows(second_contract_kernel)
        w2t = jnp.concatenate(received_rows(first_strided_kernel, 2), axis=3)
        w1t = jnp.concatenate(received_rows(first_contract_kernel), axis=1)
        wpt = jnp.concatenate(received_rows(projection_kernel), axis=1)

        (own,) = in_vmem(
            enter_kernel,
            [bounds, entry_activation],
            [((large, quarter), BF)],
            [((16 * images, quarter), BF)],
        )
        (loss,) = in_vmem(
            loss_kernel, [loss_sensitivity], [((rows, wide), BF)], [((8 * images, wide), F32)]
        )
        source = gather(own)
        z1, stats1 = in_vmem(
            functools.partial(first_kernel, chan),
            [bounds, who, *source, first_contract_kernel],
            [((large, LANES), BF), ((devices, 8, LANES), F32)],
            [((large, LANES), F32)],
        )
        got1 = exchange(stats1)
        near1 = gather(z1)
        even, zs, stats_s = in_vmem(
            functools.partial(shortcut_kernel, chan),
            [bounds, who, *source, projection_kernel],
            [((rows, depth), BF), ((rows, wide), BF), ((2 * blocks, LANES), F32)],
            [((rows, wide), F32)],
        )
        nears = gather(zs)
        a1, z2, stats2, norms1, counts = in_vmem(
            functools.partial(strided_kernel, batch, chan),
            [bounds, who, got1, *near1, tabs, first_strided_kernel, stats_s],
            [
                ((3, 2, rows + CHUNK, mid), BF),
                piece,
                ((devices, 16, LANES), F32),
                ((2 * chan, LANES), F32),
                ((8, LANES), F32),
            ],
            [((rows, LANES), F32)],
        )
        got2 = exchange(stats2)
        near2 = gather_direct(z2)
        a2, z3, stats3, norms2 = in_vmem(
            functools.partial(enlarge_kernel, batch, chan),
            [bounds, who, got2, *near2, tabs, counts, first_enlarge_kernel],
            [
                ((rows, mid), BF),
                ((rows, wide), BF),
                ((devices, 2 * blocks, LANES), F32),
                ((2 * chan, LANES), F32),
            ],
            [((rows, wide), F32)],
        )
        got3 = exchange(stats3)
        near3 = gather(z3)
        y1, y1_own, z4, stats4, norms3 = in_vmem(
            functools.partial(merge_kernel, batch, chan),
            [bounds, who, got3, got2, *near3, *nears, tabs, counts, second_contract_kernel],
            [
                ((rows, wide * chan), BF),
                ((rows, wide), F32),
                piece,
                ((devices, 8, LANES), F32),
                ((4 * blocks, LANES), F32),
            ],
            [((rows, LANES), F32)],
        )
        got4 = exchange(stats4)
        near4 = gather_direct(z4)
        a4, z5, stats5, norms4 = in_vmem(
            functools.partial(spatial_kernel, batch, chan),
            [bounds, who, got4, *near4, tabs, counts, second_spatial_kernel],
            [((rows, mid), BF), piece, ((devices, 8, LANES), F32), ((2 * chan, LANES), F32)],
            [((3, rows + 2 * CHUNK, mid), BF), ((rows, LANES), F32)],
        )
        got5 = exchange(stats5)
        near5 = gather_direct(z5)
        a5, z6, stats6, norms5 = in_vmem(
            functools.partial(last_kernel, batch, chan),
            [bounds, who, got5, *near5, tabs, counts, second_enlarge_kernel],
            [
                ((rows, mid), BF),
                ((rows, wide), F32),
                ((batch, 2 * blocks, LANES), F32),
                ((2 * chan, LANES), F32),
            ],
        )
        got6 = exchange_batch(stats6)
        result, g2, stats7, norms6 = in_vmem(
            output_kernel,
            [bounds, got6, z6, y1_own, loss, tabs, counts],
            [
                ((images, small, small, wide), BF),
                ((rows, wide), F32),
                ((batch, 2 * blocks, LANES), F32),
                ((2 * blocks, LANES), F32),
            ],
        )

        shares = [((rows, LANES), F32)] + [piece] * (chan - 1)
        routed = ((devices, 8, LANES), F32)
        got7 = exchange_batch(stats7)
        dz6, *sent, stats8, sums6 = in_vmem(
            functools.partial(back_last_kernel, batch, chan),
            [bounds, who, got7, g2, z6, norms6, tabs, counts, second_enlarge_kernel, *near5, norms5],
            [((rows, wide), BF), *shares, routed, ((2 * blocks, LANES), F32)],
            [((rows, mid), F32)],
        )
        got8 = exchange(stats8)
        parts = deliver(sent)
        expanding_grad = dot(a5, dz6, ((0,), (0,)))
        spread5, *sent, stats9, sums5 = in_vmem(
            functools.partial(back_spatial_kernel, batch, chan),
            [
                bounds, who, got8, *parts, near5[0], norms5, tabs, counts,
                second_spatial_kernel, *near4, norms4,
            ],
            [((rows, 9 * LANES), BF), *shares, routed, ((8, LANES), F32)],
            [((3, rows + 2 * CHUNK, LANES), BF), ((rows, mid), F32)],
        )
        got9 = exchange(stats9)
        parts = deliver(sent)
        middle_grad = dot(a4, spread5, ((0,), (0,)))
        dz4, sums4 = in_vmem(
            back_contract_kernel,
            [bounds, got9, *parts, near4[0], norms4, tabs, counts],
            [piece, ((8, LANES), F32)],
        )
        dz4_all = gather_direct(dz4)
        narrowing_grad = dot(y1, dz4, ((0,), (0,)))
        g1, stats10 = in_vmem(
            functools.partial(back_merge_kernel, chan),
            [bounds, *dz4_all, *w4t, g2, near3[0], nears[0], norms3, tabs],
            [((rows, wide), F32), ((batch, 4 * blocks, LANES), F32)],
            [((rows, wide), F32)],
        )
        got10 = exchange_batch(stats10)
        dz3, dzs, *sent, stats11, sums3 = in_vmem(
            functools.partial(back_enlarge_kernel, batch, chan),
            [
                bounds, who, got10, g1, near3[0], nears[0], norms3, tabs, counts,
                first_enlarge_kernel, *near2, norms2,
            ],
            [((rows, wide), BF), ((rows, wide), BF), *shares, routed, ((4 * blocks, LANES), F32)],
            [((rows, mid), F32)],
        )
        got11 = exchange(stats11)
        parts = deliver(sent)
        dzs_all = gather(dzs)
        widening_grad = dot(a2, dz3, ((0,), (0,)))
        shortcut_grad = dot(even, dzs, ((0,), (0,)))
        dz2, moved2, sums2 = in_vmem(
            back_strided_kernel,
            [bounds, got11, *parts, near2[0], norms2, tabs, counts],
            [piece, ((rows, 4 * LANES), BF), ((8, LANES), F32)],
            [((2, rows + CHUNK, LANES), BF)],
        )
        dz2_all = gather_direct(dz2)
        u1, stats12 = in_vmem(
            functools.partial(back_first_kernel, chan),
            [bounds, *dz2_all, w2t, near1[0], norms1, tabs],
            [((large, LANES), F32), ((batch, 8, LANES), F32)],
            [((2, rows + CHUNK, mid), BF), ((rows, LANES), F32)],
        )
        got12 = exchange_batch(stats12)
        taps = {}
        for p in range(2):
            for q in range(2):
                plane = a1[1 + q, 1, :rows] if p == 0 else a1[1 + q, 0, CHUNK:]
                for a, down in TAPS[p]:
                    for b, right in TAPS[q]:
                        n = 2 * down + right
                        taps[(a, b)] = dot(plane, moved2[:, n * LANES : (n + 1) * LANES], ((0,), (0,)))
        spatial_grad = jnp.stack([jnp.stack([taps[(a, b)] for b in range(3)]) for a in range(3)])
        dz1, sums1 = in_vmem(
            back_first_own_kernel,
            [bounds, got12, u1, near1[0], norms1, tabs, counts],
            [((large, LANES), BF), ((8, LANES), F32)],
        )
        dz1_all = gather(dz1)
        reducing_grad = jnp.concatenate([dot(v, dz1, ((0,), (0,))) for v in source], axis=0)
        order = jnp.arange(chan) ^ me
        reducing_grad = reducing_grad.reshape(chan, quarter, LANES)[order].reshape(depth, LANES)
        (inputs_grad,) = in_vmem(
            functools.partial(leave_kernel, chan),
            [bounds, *dz1_all, *dzs_all, w1t, wpt],
            [((images, side, side, quarter), BF)],
            [((large, quarter), F32), ((rows, quarter), F32)],
        )
        middle_grad = jnp.stack(
            [
                jnp.stack([middle_grad[:, (3 * a + b) * LANES : (3 * a + b + 1) * LANES] for b in range(3)])
                for a in range(3)
            ]
        )
        grads = [
            reducing_grad, spatial_grad, widening_grad, shortcut_grad, narrowing_grad, middle_grad, expanding_grad
        ]
        grads = [lax.psum(v.astype(BF), "batch").astype(F32) for v in grads]
        gains3, gains_s, shift3 = (sums3[n * blocks : (n + 1) * blocks].reshape(-1) for n in range(3))
        gains6, shift6 = sums6[:blocks].reshape(-1), sums6[blocks:].reshape(-1)
        return (
            result,
            inputs_grad,
            *grads,
            jnp.stack([sums1[0], sums2[0], sums4[0], sums5[0]]),
            jnp.stack([sums1[1], sums2[1], sums4[1], sums5[1]]),
            jnp.stack([gains3, gains_s, gains6]),
            jnp.stack([shift3, shift3, shift6]),
        )

    wide_act = P("batch", None, None, "chan")
    cols = P(None, "chan")
    taps = P(None, None, None, "chan")
    return jax.shard_map(
        local,
        mesh=mesh,
        in_specs=(wide_act, P("batch", None), wide_act, cols, taps, cols, cols, cols, taps)
        + (cols,) * 5,
        out_specs=(wide_act, wide_act, cols, taps, cols, cols, cols, taps) + (cols,) * 5,
        check_vma=False,
    )
```

profile of v0, /device:TPU:0, one launch (start us, length us, event | category | flops | bytes accessed | tf_op | source)
XLA Modules:
  0.0 539.1 jit_solution(17571290752371105150)
XLA Ops:
  18.2 20.6 %collective-permute-done.1.refs_2_ = bf16[1792,256]{1,0:T(8,128)(2,1)S(1)} collective-permute-done((bf16[1792,256]{1,0:T(8,128)(2,1)}, bf16[1792,256]{1,0:T(8,128)(2,1)S(1)}, u32[]{:S(2)}, u32[]{:S(2)}) %collective-permute-start.1) | collective-permute-done | bytes 917536 | tf_op jit(solution)/shard_map/ppermute | solution.py:823
  42.2 5.0 shard_map.238
  49.0 11.0 %collective-permute-done.4.refs_2_ = bf16[1792,128]{1,0:T(8,128)(2,1)S(1)} collective-permute-done((bf16[1792,128]{1,0:T(8,128)(2,1)}, bf16[1792,128]{1,0:T(8,128)(2,1)S(1)}, u32[]{:S(2)}, u32[]{:S(2)}) %collective-permute-start.4) | collective-permute-done | bytes 458784 | tf_op jit(solution)/shard_map/ppermute | solution.py:823
  60.0 6.2 %all-to-all-start = ((f32[32,8,128]{2,1,0:T(8,128)}), f32[32,8,128]{2,1,0:T(8,128)S(1)}, u32[]{:S(2)}, u32[]{:S(2)}) async-start(f32[32,8,128]{2,1,0:T(8,128)} %get-tuple-element.77), calls=%async_computation | async-start | bytes 262144 | tf_op jit(solution)/shard_map/all_to_all | solution.py:841
  77.9 7.1 %shard_map.240 = (bf16[3,2,512,512]{3,2,1,0:T(8,128)(2,1)}, bf16[448,128]{1,0:T(8,128)(2,1)}, f32[32,16,128]{2,1,0:T(8,128)}, f32[8,128]{1,0:T(8,128)}, f32[8,128]{1,0:T(8,128)}) custom-call(s32[8,2]{1,0:T(8,128)} %copy.37.bounds, s32[2]{0:T(128)} %pad_add_fusion.who, f32[32,8,128]{2,1,0:T(8,128)} %copy-done.27, ...), custom_call_target="tpu_custom_call" | custom-call | bytes 3215432 | tf_op jit(solution)/shard_map/pallas_call | solution.py:121
  111.3 8.8 %collective-permute-done.13.refs_2_ = bf16[448,512]{1,0:T(8,128)(2,1)S(1)} collective-permute-done((bf16[448,512]{1,0:T(8,128)(2,1)}, bf16[448,512]{1,0:T(8,128)(2,1)S(1)}, u32[]{:S(2)}, u32[]{:S(2)}) %collective-permute-start.13) | collective-permute-done | bytes 458784 | tf_op jit(solution)/shard_map/ppermute | solution.py:823
  124.9 8.2 %all-to-all-done.2.got3 = f32[32,8,128]{2,1,0:T(8,128)S(1)} async-done(((f32[32,8,128]{2,1,0:T(8,128)}), f32[32,8,128]{2,1,0:T(8,128)S(1)}, u32[]{:S(2)}, u32[]{:S(2)}) %all-to-all-start.2) | async-done | bytes 131104 | tf_op jit(solution)/shard_map/all_to_all | solution.py:841
  134.7 6.9 %shard_map.242 = (bf16[448,2048]{1,0:T(8,128)(2,1)}, f32[448,512]{1,0:T(8,128)}, bf16[448,128]{1,0:T(8,128)(2,1)}, f32[32,8,128]{2,1,0:T(8,128)}, f32[16,128]{1,0:T(8,128)}) custom-call(s32[8,2]{1,0:T(8,128)} %copy.37.bounds, s32[2]{0:T(128)} %pad_add_fusion.who, f32[32,8,128]{2,1,0:T(8,128)} %copy-done.25, f32[32,16,128]{2,1,0:T(8,128)} %copy-done.11, ...), custom_call_target="tpu_custom_call" | custom-call | bytes 4657224 | tf_op jit(solution)/shard_map/pallas_call | solution.py:121
  146.3 5.3 collective-permute-done.19.refs_2_.refs_11_
  173.6 11.2 %collective-permute-done.22.refs_2_ = bf16[448,128]{1,0:T(8,128)(2,1)S(1)} collective-permute-done((bf16[448,128]{1,0:T(8,128)(2,1)S(1)}, bf16[448,128]{1,0:T(8,128)(2,1)S(1)}, u32[]{:S(2)}, u32[]{:S(2)}) %collective-permute-start.22) | collective-permute-done | bytes 114720 | tf_op jit(solution)/shard_map/ppermute | solution.py:823
  192.2 4.9 all-to-all-start.5
  197.2 6.7 %all-to-all-done.5.got = f32[8,8,128]{2,1,0:T(8,128)S(1)} async-done(((f32[8,8,128]{2,1,0:T(8,128)}), f32[8,8,128]{2,1,0:T(8,128)S(1)}, u32[]{:S(2)}, u32[]{:S(2)}) %all-to-all-start.5) | async-done | bytes 32800 | tf_op jit(solution)/shard_map/all_to_all | solution.py:844
  213.7 5.4 %all-to-all-done.6.got = f32[8,8,128]{2,1,0:T(8,128)S(1)} async-done(((f32[8,8,128]{2,1,0:T(8,128)}), f32[8,8,128]{2,1,0:T(8,128)S(1)}, u32[]{:S(2)}, u32[]{:S(2)}) %all-to-all-start.6) | async-done | bytes 32800 | tf_op jit(solution)/shard_map/all_to_all | solution.py:844
  237.7 5.6 %shard_map.248 = (bf16[448,1152]{1,0:T(8,128)(2,1)}, f32[448,128]{1,0:T(8,128)}, bf16[448,128]{1,0:T(8,128)(2,1)}, bf16[448,128]{1,0:T(8,128)(2,1)}, bf16[448,12...) custom-call(s32[8,2]{1,0:T(8,128)} %copy.37.bounds, s32[2]{0:T(128)} %pad_add_fusion.who, ...), custom_call_target="tpu_custom_call" | custom-call | bytes 2535496 | tf_op jit(solution)/shard_map/pallas_call | solution.py:121
  267.2 4.9 shard_map.250
  277.1 5.2 all-to-all-done.9.got
  282.9 5.0 shard_map.251
  314.2 6.4 %shard_map.253 = (f32[1792,128]{1,0:T(8,128)}, f32[8,8,128]{2,1,0:T(8,128)}) custom-call(s32[8,2]{1,0:T(8,128)} %copy.37.bounds, bf16[448,128]{1,0:T(8,128)(2,1)} %get-tuple-element.119.refs_0_, bf16[448,128]{1,0:T(8,128)(2,1)} %copy-done.71, bf16[448,128]{1,0:T(8,128)(2,1)} %copy-done.73, bf16[448,128]{1,0:T(8,128)(2,1)} %copy-done.76, ...), custom_call_target="tpu_custom_call" | custom-call | bytes 2166848 | tf_op jit(solution)/shard_map/pallas_call | solution.py:121
  325.4 5.2 all-to-all-done.11.got
  344.3 12.4 %collective-permute-done.52 = bf16[256,128]{1,0:T(8,128)(2,1)S(1)} collective-permute-done((bf16[256,128]{1,0:T(8,128)(2,1)S(1)}, bf16[256,128]{1,0:T(8,128)(2,1)S(1)}, u32[]{:S(2)}, u32[]{:S(2)}) %collective-permute-start.52) | collective-permute-done | bytes 65568 | tf_op jit(solution)/shard_map/ppermute | solution.py:823
  364.6 9.5 %collective-permute-done.49.refs_6_ = bf16[448,512]{1,0:T(8,128)(2,1)S(1)} collective-permute-done((bf16[448,512]{1,0:T(8,128)(2,1)S(1)}, bf16[448,512]{1,0:T(8,128)(2,1)S(1)}, u32[]{:S(2)}, u32[]{:S(2)}) %collective-permute-start.49) | collective-permute-done | bytes 458784 | tf_op jit(solution)/shard_map/ppermute | solution.py:823
  374.1 9.5 %collective-permute-done.46.refs_2_ = bf16[1792,128]{1,0:T(8,128)(2,1)S(1)} collective-permute-done((bf16[1792,128]{1,0:T(8,128)(2,1)S(1)}, bf16[1792,128]{1,0:T(8,128)(2,1)S(1)}, u32[]{:S(2)}, u32[]{:S(2)}) %collective-permute-start.46) | collective-permute-done | bytes 458784 | tf_op jit(solution)/shard_map/ppermute | solution.py:823
  387.6 7.1 %shard_map.255 = bf16[8,14,14,256]{3,2,1,0:T(8,128)(2,1)} custom-call(s32[8,2]{1,0:T(8,128)} %copy.37.bounds, bf16[1792,128]{1,0:T(8,128)(2,1)} %get-tuple-element.123.refs_0_, bf16[1792,128]{1,0:T(8,128)(2,1)} %copy-done.33, bf16[1792,128]{1,0:T(8,128)(2,1)} %copy-done.30, bf16[1792,128]{1,0:T(8,128)(2,1)} %copy-done.37, ...), custom_call_target="tpu_custom_call" | custom-call | bytes 4980800 | tf_op jit(solution)/shard_map/pallas_call | solution.py:121
  397.2 124.9 %all-reduce.3.cloned.1.call-done = (bf16[1024,128]{1,0:T(8,128)(2,1)}, bf16[3,3,512,128]{3,2,1,0:T(8,128)(2,1)}, bf16[512,512]{1,0:T(8,128)(2,1)}, bf16[1024,512...) async-done(((bf16[1024,128]{1,0:T(8,128)(2,1)}, bf16[3,3,512,128]{3,2,1,0:T(8,128)(2,1)}, ...) | async-done | bytes 5242896 | tf_op jit(solution)/shard_map/psum | solution.py:1089
  (382 shorter events, 220.9 us)
Async XLA Ops:
  15.3 23.5 %collective-permute-start.1 = (bf16[1792,256]{1,0:T(8,128)(2,1)}, bf16[1792,256]{1,0:T(8,128)(2,1)S(1)}, u32[]{:S(2)}, u32[]{:S(2)}) collective-permute-start(bf16[1792,256]{1,0:T(8,128)(2,1)} %shard_map.237.refs_0_), channel_id=1, source_target_pairs={{0,2},{1,3},{2,0},{3,1},{4,6},{5,7},{6,4},{7,5},{8,10},{9,11},{10,... | collective-permute-start | bytes 2752520 | tf_op jit(solution)/shard_map/ppermute | solution.py:823
  18.2 21.2 %collective-permute-start = (bf16[1792,256]{1,0:T(8,128)(2,1)}, bf16[1792,256]{1,0:T(8,128)(2,1)S(1)}, u32[]{:S(2)}, u32[]{:S(2)}) collective-permute-start(bf16[1792,256]{1,0:T(8,128)(2,1)} %shard_map.237.refs_0_), channel_id=1, source_target_pairs={{0,1},{1,0},{2,3},{3,2},{4,5},{5,4},{6,7},{7,6},{8,9},{9,8},{10,11... | collective-permute-start | bytes 2752520 | tf_op jit(solution)/shard_map/ppermute | solution.py:823
  49.0 28.0 %collective-permute-start.3 = (bf16[1792,128]{1,0:T(8,128)(2,1)}, bf16[1792,128]{1,0:T(8,128)(2,1)S(1)}, u32[]{:S(2)}, u32[]{:S(2)}) collective-permute-start(bf16[1792,128]{1,0:T(8,128)(2,1)} %get-tuple-element.78.refs_0_.refs_5_.near), channel_id=1, source_target_pairs={{0,1},{1,0},{2,3},{3,2},{4,5},{5,4},{6,7},{7,6},{8,9},{9,8},{10,11... | collective-permute-start | bytes 1376264 | tf_op jit(solution)/shard_map/ppermute | solution.py:823
  60.0 17.0 %collective-permute-start.5 = (bf16[1792,128]{1,0:T(8,128)(2,1)S(1)}, bf16[1792,128]{1,0:T(8,128)(2,1)S(1)}, u32[]{:S(2)}, u32[]{:S(2)}) collective-permute-start(bf16[1792,128]{1,0:T(8,128)(2,1)S(1)} %collective-permute-done.4.refs_2_), channel_id=1, source_target_pairs={{0,1},{1,0},{2,3},{3,2},{4,5},{5,4},{6,7},{7,6},{8,9},{9,8},{10,11... | collective-permute-start | bytes 1376264 | tf_op jit(solution)/shard_map/ppermute | solution.py:823
  60.0 16.9 %all-to-all-start = ((f32[32,8,128]{2,1,0:T(8,128)}), f32[32,8,128]{2,1,0:T(8,128)S(1)}, u32[]{:S(2)}, u32[]{:S(2)}) async-start(f32[32,8,128]{2,1,0:T(8,128)} %get-tuple-element.77), calls=%async_computation | async-start | bytes 262144 | tf_op jit(solution)/shard_map/all_to_all | solution.py:841
  85.0 15.5 %all-to-all-start.1 = ((f32[32,16,128]{2,1,0:T(8,128)}), f32[32,16,128]{2,1,0:T(8,128)S(1)}, u32[]{:S(2)}, u32[]{:S(2)}) async-start(f32[32,16,128]{2,1,0:T(8,128)} %get-tuple-element.80), calls=%async_computation.1 | async-start | bytes 524288 | tf_op jit(solution)/shard_map/all_to_all | solution.py:841
  92.1 18.7 %collective-permute-start.16 = (bf16[448,512]{1,0:T(8,128)(2,1)S(1)}, bf16[448,512]{1,0:T(8,128)(2,1)S(1)}, u32[]{:S(2)}, u32[]{:S(2)}) collective-permute-start(bf16[448,512]{1,0:T(8,128)(2,1)S(1)} %copy-done.10), channel_id=1, source_target_pairs={{0,2},{1,3},{2,0},{3,1},{4,6},{5,7},{6,4},{7,5},{8,10},{9,11},{10,... | collective-permute-start | bytes 1376264 | tf_op jit(solution)/shard_map/ppermute | solution.py:823
  105.6 19.3 %collective-permute-start.15 = (bf16[448,512]{1,0:T(8,128)(2,1)S(1)}, bf16[448,512]{1,0:T(8,128)(2,1)S(1)}, u32[]{:S(2)}, u32[]{:S(2)}) collective-permute-start(bf16[448,512]{1,0:T(8,128)(2,1)S(1)} %copy-done.10), channel_id=1, source_target_pairs={{0,1},{1,0},{2,3},{3,2},{4,5},{5,4},{6,7},{7,6},{8,9},{9,8},{10,11... | collective-permute-start | bytes 1376264 | tf_op jit(solution)/shard_map/ppermute | solution.py:823
  110.8 22.3 %collective-permute-start.12 = (bf16[448,512]{1,0:T(8,128)(2,1)}, bf16[448,512]{1,0:T(8,128)(2,1)S(1)}, u32[]{:S(2)}, u32[]{:S(2)}) collective-permute-start(bf16[448,512]{1,0:T(8,128)(2,1)} %get-tuple-element.84.refs_0_.refs_9_.near3), channel_id=1, source_target_pairs={{0,1},{1,0},{2,3},{3,2},{4,5},{5,4},{6,7},{7,6},{8,9},{9,8},{10,11... | collective-permute-start | bytes 1376264 | tf_op jit(solution)/shard_map/ppermute | solution.py:823
  159.4 28.4 %all-to-all-start.4 = ((f32[32,8,128]{2,1,0:T(8,128)}), f32[32,8,128]{2,1,0:T(8,128)S(1)}, u32[]{:S(2)}, u32[]{:S(2)}) async-start(f32[32,8,128]{2,1,0:T(8,128)} %get-tuple-element.88), calls=%async_computation.4 | async-start | bytes 262144 | tf_op jit(solution)/shard_map/all_to_all | solution.py:841
  165.2 47.3 %collective-permute-start.42 = (bf16[3,3,128,128]{3,2,1,0:T(8,128)(2,1)}, bf16[3,3,128,128]{3,2,1,0:T(8,128)(2,1)S(1)}, u32[]{:S(2)}, u32[]{:S(2)}) collective-permute-start(bf16[3,3,128,128]{3,2,1,0:T(8,128)(2,1)} %get-tuple-element.171), channel_id=1, source_target_pairs={{0,1},{1,0},{2,3},{3,2},{4,5},{5,4},{6,7},{7,6},{8,9},{9,8},{10,11... | collective-permute-start | bytes 884744 | tf_op jit(solution)/shard_map/ppermute | solution.py:823
  165.4 47.1 %collective-permute-start.43 = (bf16[3,3,128,128]{3,2,1,0:T(8,128)(2,1)S(1)}, bf16[3,3,128,128]{3,2,1,0:T(8,128)(2,1)S(1)}, u32[]{:S(2)}, u32[]{:S(2)}) collective-permute-start(bf16[3,3,128,128]{3,2,1,0:T(8,128)(2,1)S(1)} %get-tuple-element.173), channel_id=1, source_target_pairs={{0,2},{1,3},{2,0},{3,1},{4,6},{5,7},{6,4},{7,5},{8,10},{9,11},{10,... | collective-permute-start | bytes 884744 | tf_op jit(solution)/shard_map/ppermute | solution.py:823
  167.1 45.4 %collective-permute-start.44 = (bf16[3,3,128,128]{3,2,1,0:T(8,128)(2,1)S(1)}, bf16[3,3,128,128]{3,2,1,0:T(8,128)(2,1)S(1)}, u32[]{:S(2)}, u32[]{:S(2)}) collective-permute-start(bf16[3,3,128,128]{3,2,1,0:T(8,128)(2,1)S(1)} %get-tuple-element.172), channel_id=1, source_target_pairs={{0,3},{1,2},{2,1},{3,0},{4,7},{5,6},{6,5},{7,4},{8,11},{9,10},{10,... | collective-permute-start | bytes 884744 | tf_op jit(solution)/shard_map/ppermute | solution.py:823
  167.1 17.6 %collective-permute-start.22 = (bf16[448,128]{1,0:T(8,128)(2,1)S(1)}, bf16[448,128]{1,0:T(8,128)(2,1)S(1)}, u32[]{:S(2)}, u32[]{:S(2)}) collective-permute-start(bf16[448,128]{1,0:T(8,128)(2,1)S(1)} %copy-done.17), channel_id=1, source_target_pairs={{0,2},{1,3},{2,0},{3,1},{4,6},{5,7},{6,4},{7,5},{8,10},{9,11},{10,... | collective-permute-start | bytes 344072 | tf_op jit(solution)/shard_map/ppermute | solution.py:823
  168.8 17.6 %collective-permute-start.23 = (bf16[448,128]{1,0:T(8,128)(2,1)S(1)}, bf16[448,128]{1,0:T(8,128)(2,1)S(1)}, u32[]{:S(2)}, u32[]{:S(2)}) collective-permute-start(bf16[448,128]{1,0:T(8,128)(2,1)S(1)} %copy-done.17), channel_id=1, source_target_pairs={{0,3},{1,2},{2,1},{3,0},{4,7},{5,6},{6,5},{7,4},{8,11},{9,10},{10,... | collective-permute-start | bytes 344072 | tf_op jit(solution)/shard_map/ppermute | solution.py:823
  184.8 74.7 %collective-permute-start.33 = (bf16[512,128]{1,0:T(8,128)(2,1)}, bf16[512,128]{1,0:T(8,128)(2,1)S(1)}, u32[]{:S(2)}, u32[]{:S(2)}) collective-permute-start(bf16[512,128]{1,0:T(8,128)(2,1)} %get-tuple-element.179), channel_id=1, source_target_pairs={{0,1},{1,0},{2,3},{3,2},{4,5},{5,4},{6,7},{7,6},{8,9},{9,8},{10,11... | collective-permute-start | bytes 393224 | tf_op jit(solution)/shard_map/ppermute | solution.py:823
  186.5 75.5 %collective-permute-start.34 = (bf16[512,128]{1,0:T(8,128)(2,1)}, bf16[512,128]{1,0:T(8,128)(2,1)S(1)}, u32[]{:S(2)}, u32[]{:S(2)}) collective-permute-start(bf16[512,128]{1,0:T(8,128)(2,1)} %get-tuple-element.181), channel_id=1, source_target_pairs={{0,2},{1,3},{2,0},{3,1},{4,6},{5,7},{6,4},{7,5},{8,10},{9,11},{10,... | collective-permute-start | bytes 393224 | tf_op jit(solution)/shard_map/ppermute | solution.py:823
  324.0 198.1 %all-reduce.3.cloned.1.call-start = ((), (), s32[]{:S(2)}) async-start(), calls=%async_computation.12 | async-start | bytes 10485760 | tf_op jit(solution)/shard_map/psum | solution.py:1089
  340.4 17.5 %collective-permute-start.54 = (bf16[256,512]{1,0:T(8,128)(2,1)S(1)}, bf16[256,512]{1,0:T(8,128)(2,1)S(1)}, u32[]{:S(2)}, u32[]{:S(2)}) collective-permute-start(bf16[256,512]{1,0:T(8,128)(2,1)S(1)} %get-tuple-element.175), channel_id=1, source_target_pairs={{0,1},{1,0},{2,3},{3,2},{4,5},{5,4},{6,7},{7,6},{8,9},{9,8},{10,11... | collective-permute-start | bytes 786440 | tf_op jit(solution)/shard_map/ppermute | solution.py:823
  340.5 17.4 %collective-permute-start.55 = (bf16[256,512]{1,0:T(8,128)(2,1)S(1)}, bf16[256,512]{1,0:T(8,128)(2,1)S(1)}, u32[]{:S(2)}, u32[]{:S(2)}) collective-permute-start(bf16[256,512]{1,0:T(8,128)(2,1)S(1)} %get-tuple-element.177), channel_id=1, source_target_pairs={{0,2},{1,3},{2,0},{3,1},{4,6},{5,7},{6,4},{7,5},{8,10},{9,11},{10,... | collective-permute-start | bytes 786440 | tf_op jit(solution)/shard_map/ppermute | solution.py:823
  341.0 16.9 %collective-permute-start.56 = (bf16[256,512]{1,0:T(8,128)(2,1)S(1)}, bf16[256,512]{1,0:T(8,128)(2,1)S(1)}, u32[]{:S(2)}, u32[]{:S(2)}) collective-permute-start(bf16[256,512]{1,0:T(8,128)(2,1)S(1)} %get-tuple-element.176), channel_id=1, source_target_pairs={{0,3},{1,2},{2,1},{3,0},{4,7},{5,6},{6,5},{7,4},{8,11},{9,10},{10,... | collective-permute-start | bytes 786440 | tf_op jit(solution)/shard_map/ppermute | solution.py:823
  361.2 22.4 %collective-permute-start.46 = (bf16[1792,128]{1,0:T(8,128)(2,1)S(1)}, bf16[1792,128]{1,0:T(8,128)(2,1)S(1)}, u32[]{:S(2)}, u32[]{:S(2)}) collective-permute-start(bf16[1792,128]{1,0:T(8,128)(2,1)S(1)} %copy-done.1), channel_id=1, source_target_pairs={{0,2},{1,3},{2,0},{3,1},{4,6},{5,7},{6,4},{7,5},{8,10},{9,11},{10,... | collective-permute-start | bytes 1376264 | tf_op jit(solution)/shard_map/ppermute | solution.py:823
  363.5 22.3 %collective-permute-start.48 = (bf16[448,512]{1,0:T(8,128)(2,1)S(1)}, bf16[448,512]{1,0:T(8,128)(2,1)S(1)}, u32[]{:S(2)}, u32[]{:S(2)}) collective-permute-start(bf16[448,512]{1,0:T(8,128)(2,1)S(1)} %copy-done.28), channel_id=1, source_target_pairs={{0,1},{1,0},{2,3},{3,2},{4,5},{5,4},{6,7},{7,6},{8,9},{9,8},{10,11... | collective-permute-start | bytes 1376264 | tf_op jit(solution)/shard_map/ppermute | solution.py:823
  364.2 21.5 %collective-permute-start.45 = (bf16[1792,128]{1,0:T(8,128)(2,1)S(1)}, bf16[1792,128]{1,0:T(8,128)(2,1)S(1)}, u32[]{:S(2)}, u32[]{:S(2)}) collective-permute-start(bf16[1792,128]{1,0:T(8,128)(2,1)S(1)} %copy-done.1), channel_id=1, source_target_pairs={{0,1},{1,0},{2,3},{3,2},{4,5},{5,4},{6,7},{7,6},{8,9},{9,8},{10,11... | collective-permute-start | bytes 1376264 | tf_op jit(solution)/shard_map/ppermute | solution.py:823
  (138 other events, 1069.6 us)
Sparse Core Ops, SparseCore 0:
  339.2 182.7 all-reduce.2
where the time goes:
time: 541 us; the launch traced here: 539 us
  waiting for transfers between devices  283 us (52%)
  Pallas kernels  89.3 us (17%)
  starting transfers between devices  83.1 us (15%)
  local copies, waits for them, and re-layouts  29 us (5%)
  matrix products  21.1 us (4%)
  other arithmetic  18.3 us (3%)
  between operations  15.1 us (3%)
    psum x1, waiting for transfers between devices, local(): grads = [lax.psum(v.astype(BF), 'batch').astype(F32) for v in grads]  125 us
    ppermute x57, waiting for transfers between devices, swap(): lax.ppermute(v, axis, [(k, k ^ mask) for k in range(mesh.shape[axis])])  114 us
    pallas_call x19, Pallas kernels, in_vmem(): pl.pallas_call(kernel, out_shape=[jax.ShapeDtypeStruct(s, d) for s, d in...  89.3 us
    ppermute x57, starting transfers between devices, swap(): lax.ppermute(v, axis, [(k, k ^ mask) for k in range(mesh.shape[axis])])  36.5 us
    all_to_all x8, starting transfers between devices, exchange(): return lax.all_to_all(stats, everyone, 0, 0)  31.3 us
    unnamed x189, local copies, waits for them, and re-layouts  22.8 us
    all_to_all x4, waiting for transfers between devices, exchange_batch(): return lax.all_to_all(stats, 'batch', 0, 0)  22.5 us
    all_to_all x8, waiting for transfers between devices, exchange(): return lax.all_to_all(stats, everyone, 0, 0)  22 us
  transfers between devices with their start and end apart: 70, of which 31 were waited for; matrix products, arithmetic and copies ran while one was open for 6% of the time, Pallas kernels for 7%

commit v1 on v0

v1 whole, which is shorter than its diff:
```python
import functools
import math

import jax
import jax.numpy as jnp
from jax import lax
from jax.experimental import pallas as pl
from jax.experimental.pallas import tpu as pltpu
from jax.sharding import PartitionSpec as P

EPS = 1e-05
BF = jnp.bfloat16
F32 = jnp.float32
GELU_A = 0.7978845608028654
GELU_B = 0.044715
LANES = 128
MID = 512
SIDE = 14
IMAGES = 8
CELLS = 8
CHUNK = CELLS * IMAGES
LINE = SIDE * IMAGES
VMEM_LIMIT = 20 * 1024 * 1024


def dot(a, b, dims=((1,), (0,))):
    return lax.dot_general(a, b, (dims, ((), ())), preferred_element_type=F32)


def gelu(v):
    return 0.5 * v * (1.0 + jnp.tanh(GELU_A * v * (1.0 + GELU_B * v * v)))


def gelu_slope(v):
    square = v * v
    t = jnp.tanh(GELU_A * v * (1.0 + GELU_B * square))
    return 0.5 * (1.0 + t) * (1.0 + v * (1.0 - t) * (GELU_A + 3.0 * GELU_A * GELU_B * square))


class Masks:
    def __init__(self, info):
        image = lax.broadcasted_iota(jnp.int32, (IMAGES, LANES), 0)
        high = jnp.zeros((IMAGES, LANES), jnp.int32)
        low = jnp.zeros((IMAGES, LANES), jnp.int32)
        inside = jnp.int32(0)
        outside = jnp.int32(0)
        for n in range(IMAGES):
            h, w = info[2 + n], info[2 + IMAGES + n]
            high = jnp.where(image == n, h, high)
            low = jnp.where(image == n, w, low)
            inside = inside + h * w
            outside = outside + lax.shift_right_logical(h + 1, 1) * lax.shift_right_logical(w + 1, 1)
        self.high = high[None]
        self.low = low[None]
        self.column = lax.broadcasted_iota(jnp.int32, (2 * CELLS, IMAGES, LANES), 0)
        self.local_in = inside.astype(F32)
        self.local_out = outside.astype(F32)

    def large(self, row):
        return (row < self.high) & (self.column[:SIDE] < self.low)

    def small(self, row):
        return (2 * row < self.high) & (2 * self.column[:CELLS] < self.low)


def keep(mask, value):
    return jnp.where(mask, value, 0.0)


def cube(rows):
    return rows.astype(F32).reshape(-1, IMAGES, LANES)


def flat(value):
    return value.reshape(-1, LANES)


def padded(value):
    return jnp.concatenate([value, jnp.zeros((1,) + value.shape[1:], F32)], axis=0)


def parted(value):
    pairs = value.reshape(CELLS - 1, 2, *value.shape[1:])
    return padded(pairs[:, 0]), padded(pairs[:, 1])


def merged(even, odd):
    pairs = jnp.stack([even[: CELLS - 1], odd[: CELLS - 1]], axis=1)
    return pairs.reshape(SIDE, *even.shape[1:])


def total_of(value):
    return jnp.sum(value, axis=0)


def row_sum(value):
    return jnp.sum(value, axis=0, keepdims=True)


def at(step, size):
    return pl.ds(pl.multiple_of(step * size, size), size)


def lane_block(index, width=LANES):
    return pl.ds(pl.multiple_of(index * width, width), width)


def push_left(value):
    return jnp.concatenate([value[1:], jnp.zeros((1, IMAGES, LANES), F32)], axis=0)


def push_right(value):
    return jnp.concatenate([jnp.zeros((1, IMAGES, LANES), F32), value[:-1]], axis=0)


def norm_of(got, info, batch, chan, k, row, local, count):
    column = info[0] ^ k
    total = got[column]
    for n in range(1, batch):
        total = total + got[n * chan + column]
    mine = got[info[1] * chan + column]
    mean = total[row : row + 1] / count
    inverse = lax.rsqrt(total[row + 1 : row + 2] / count - mean * mean + EPS)
    return mine[row : row + 1] / local - mean, inverse


def whole(got):
    total = got[0]
    for n in range(1, got.shape[0]):
        total = total + got[n]
    return total


class Late:
    def __init__(self, source, held, semaphore):
        self.copy = pltpu.make_async_copy(source, held, semaphore)
        self.held = held
        self.waiting = True
        self.copy.start()

    def use(self):
        if self.waiting:
            self.copy.wait()
            self.waiting = False
        return self.held


class Far:
    def __init__(self, held, target, semaphore):
        self.copy = pltpu.make_async_copy(held, target, semaphore)
        self.held = held
        self.sent = False
        self.shape = held.shape
        self.dtype = held.dtype

    def __getitem__(self, place):
        return self.held[place]

    def __setitem__(self, place, value):
        self.held[place] = value

    def send(self):
        self.sent = True
        self.copy.start()


def ready(value):
    if isinstance(value, (list, tuple)):
        return [ready(v) for v in value]
    return value.use() if isinstance(value, Late) else value


class far:
    def __init__(self, value):
        self.value = value


def fars(values):
    return [far(v) for v in values]


def in_vmem(kernel, ins, outs, scratch=(), after=(), save=()):
    anywhere = pl.BlockSpec(memory_space=pl.ANY)
    inside = pl.BlockSpec(memory_space=pltpu.VMEM)
    args = [pltpu.with_memory_space_constraint(v, pltpu.HBM) for v in after]
    specs, late, buffers = [anywhere] * len(after), [], []
    for n, v in enumerate(ins):
        if isinstance(v, far):
            late.append(n)
            buffers.append(pltpu.VMEM(v.value.shape, v.value.dtype))
            args.append(pltpu.with_memory_space_constraint(v.value, pltpu.HBM))
            specs.append(anywhere)
        elif v.dtype == jnp.int32:
            args.append(v)
            specs.append(pl.BlockSpec(memory_space=pltpu.SMEM))
        else:
            args.append(pltpu.with_memory_space_constraint(v, pltpu.VMEM))
            specs.append(inside)
    distant = [n for n, out in enumerate(outs) if len(out) > 2]
    buffers += [pltpu.VMEM(*outs[n][:2]) for n in distant]
    shapes = [(pltpu.HBM if len(out) > 2 else pltpu.VMEM)(*out[:2]) for out in outs]
    shapes += [pltpu.HBM(ins[n].shape, ins[n].dtype) for n in save]
    out_specs = [anywhere if len(out) > 2 else inside for out in outs] + [anywhere] * len(save)
    semaphores = len(buffers) + len(save)

    def body(*refs):
        refs = list(refs[len(after) :])
        given, refs = refs[: len(ins)], refs[len(ins) :]
        made, refs = refs[: len(outs)], refs[len(outs) :]
        saved, refs = refs[: len(save)], refs[len(save) :]
        free, refs = refs[: len(scratch)], refs[len(scratch) :]
        held, marks = refs[: len(buffers)], refs[len(buffers) :]
        for place, n in enumerate(late):
            given[n] = Late(given[n], held[place], marks[place])
        for place, n in enumerate(distant, len(late)):
            made[n] = Far(held[place], made[n], marks[place])
        copies = [
            pltpu.make_async_copy(given[n], out, mark)
            for n, out, mark in zip(save, saved, marks[len(buffers) :])
        ]
        for copy in copies:
            copy.start()
        kernel(*given, *made, *free)
        for n in distant:
            if not made[n].sent:
                made[n].send()
        for n in late:
            given[n].use()
        for n in distant:
            made[n].copy.wait()
        for copy in copies:
            copy.wait()

    return pl.pallas_call(
        body,
        out_shape=shapes,
        in_specs=specs,
        out_specs=out_specs,
        scratch_shapes=[pltpu.VMEM(*v) for v in scratch] + buffers + [pltpu.SemaphoreType.DMA] * semaphores,
        compiler_params=pltpu.CompilerParams(vmem_limit_bytes=VMEM_LIMIT),
        cost_estimate=pl.CostEstimate(flops=4 * 10**9, bytes_accessed=0, transcendentals=0),
    )(*args)


def sums_of(z, chunks, lanes, mask=None, size=CHUNK):
    def step(t, carry):
        value = cube(z[at(t, size), lanes])
        if mask is not None:
            value = keep(mask(t), value)
        return carry[0] + total_of(value), carry[1] + total_of(value * value)

    zero = jnp.zeros((IMAGES, LANES), F32)
    total, squares = lax.fori_loop(0, chunks, step, (zero, zero))
    return row_sum(total), row_sum(squares)


def centre_into(out, z, chunks, lanes, mean, size=CHUNK):
    def step(t, _):
        out[at(t, size), lanes] = (z[at(t, size), lanes] - mean).astype(BF)
        return 0

    lax.fori_loop(0, chunks, step, 0)


def broadcast_rows(out, rows):
    block = jnp.concatenate(
        list(rows) + [jnp.zeros((out.shape[1] - len(rows), LANES), F32)]
        if len(rows) < out.shape[1]
        else list(rows),
        axis=0,
    )
    out[...] = jnp.broadcast_to(block[None], out.shape)


def fill_rows(out, rows):
    for n, row in enumerate(rows):
        out[n : n + 1, :] = row
    if len(rows) < out.shape[0]:
        out[len(rows) :, :] = jnp.zeros((out.shape[0] - len(rows), LANES), F32)


def enter_kernel(info, x, out):
    masks = Masks(info)

    def step(r, _):
        mask = masks.large(r)
        for q in range(x.shape[3] // LANES):
            lanes = slice(q * LANES, (q + 1) * LANES)
            out[at(r, LINE), lanes] = flat(keep(mask, x[r, :, :, lanes].astype(F32))).astype(BF)
        return 0

    lax.fori_loop(0, SIDE, step, 0)


def first_kernel(chan, w, info, *refs):
    source, (zc, stats, z) = refs[:chan], refs[chan:]
    masks = Masks(info)
    rows, depth = source[0].shape
    part = 2 * LINE
    w = w.use()

    def step(t, _):
        total = None
        for k in range(chan):
            term = dot(source[k][at(t, part), :], w[at(info[0] ^ k, depth), :])
            total = term if total is None else total + term
        z[at(t, part), :] = total
        return 0

    lax.fori_loop(0, rows // part, step, 0)
    total, squares = sums_of(z, SIDE, slice(0, LANES), size=LINE)
    ones = jnp.ones((1, LANES), F32)
    broadcast_rows(stats, (total, squares, ones * masks.local_in, ones * masks.local_out))
    centre_into(zc, z, SIDE, slice(0, LANES), total / masks.local_in, LINE)


def shortcut_kernel(chan, w, info, *refs):
    source, (even, zc, stats, z) = refs[:chan], refs[chan:]
    masks = Masks(info)
    rows, width = z.shape
    depth = source[0].shape[1]
    chunks = rows // CHUNK

    def step(i, _):
        for k in range(chan):
            for q in range(depth // LANES):
                lanes = slice(q * LANES, (q + 1) * LANES)
                value, _ = parted(cube(source[k][at(2 * i, LINE), lanes]))
                place = lane_block((info[0] ^ k) * (depth // LANES) + q)
                even[at(i, CHUNK), place] = flat(value).astype(BF)
        return 0

    lax.fori_loop(0, chunks, step, 0)
    even.send()
    z[...] = dot(even[...], w.use()[...])
    blocks = width // LANES
    for q in range(blocks):
        lanes = slice(q * LANES, (q + 1) * LANES)
        total, squares = sums_of(z, chunks, lanes)
        stats[q : q + 1, :] = total
        stats[blocks + q : blocks + q + 1, :] = squares
        centre_into(zc, z, chunks, lanes, total / masks.local_out)


def first_act_kernel(batch, chan, pair, info, got, *refs):
    near, (tabs, *outs, norms, counts) = refs[: len(pair)], refs[len(pair) :]
    masks = Masks(info)
    total = whole(got)
    count_in, count_out = total[2:3] / chan, total[3:4] / chan
    fill_rows(counts, (count_in, count_out))
    params = [norm_of(got, info, batch, chan, k, 0, masks.local_in, count_in) for k in pair]
    norms[0:1, :] = params[0][0]
    norms[1:2, :] = params[0][1]

    def step(r, _):
        mask = masks.large(r)
        for n, k in enumerate(pair):
            scale = params[n][1] * tabs[k, 0:1, :]
            shift = params[n][0] * scale + tabs[k, 4:5, :]
            value = keep(mask, gelu(cube(near[n][at(r, LINE), :]) * scale + shift))
            outs[n][at(r, LINE), :] = flat(value).astype(BF)
        return 0

    lax.fori_loop(0, SIDE, step, 0)


def strided_kernel(chan, w, info, *refs):
    pieces, (extra, a, zc, stats, z) = refs[:chan], refs[chan:]
    masks = Masks(info)
    width = a.shape[3]
    for tap in range(3):
        a[tap, 0, 0:CHUNK, :] = jnp.zeros((CHUNK, width), BF)

    def step(r, _):
        line = r + 1
        half, place = line & 1, lax.shift_right_logical(line, 1)
        for k in range(chan):
            lanes = lane_block(info[0] ^ k)
            even, odd = parted(cube(pieces[k][at(r, LINE), :]))
            a[0, half, at(place, CHUNK), lanes] = flat(push_right(odd)).astype(BF)
            a[1, half, at(place, CHUNK), lanes] = flat(even).astype(BF)
            a[2, half, at(place, CHUNK), lanes] = flat(odd).astype(BF)
        return 0

    lax.fori_loop(0, SIDE, step, 0)
    a.send()
    rows = z.shape[0]
    acc = None
    w = w.use()
    for i, (half, first) in enumerate(((0, 0), (1, 0), (0, CHUNK))):
        for j in range(3):
            term = dot(a[j, half, first : first + rows, :], w[i, j])
            acc = term if acc is None else acc + term
    z[...] = acc
    chunks = rows // CHUNK
    total, squares = sums_of(z, chunks, slice(0, LANES), masks.small)
    block = jnp.concatenate([total, squares, jnp.zeros((6, LANES), F32), extra[...]], axis=0)
    stats[...] = jnp.broadcast_to(block[None], stats.shape)
    centre_into(zc, z, chunks, slice(0, LANES), total / masks.local_out)


def activate_into(near, params, tabs, gain, chan, info, masks, chunks, store):
    def step(t, _):
        mask = masks.small(t)
        for k in range(chan):
            scale = params[k][1] * tabs[k, gain : gain + 1, :]
            shift = params[k][0] * scale + tabs[k, gain + 4 : gain + 5, :]
            value = keep(mask, gelu(cube(near[k][at(t, CHUNK), :]) * scale + shift))
            store(t, lane_block(info[0] ^ k), value)
        return 0

    lax.fori_loop(0, chunks, step, 0)


def store_norms(norms, params):
    for k, norm in enumerate(params):
        norms[2 * k : 2 * k + 1, :] = norm[0]
        norms[2 * k + 1 : 2 * k + 2, :] = norm[1]


def enlarge_kernel(batch, chan, w, info, got, *refs):
    near, (tabs, counts, a, zc, stats, norms, z) = refs[:chan], refs[chan:]
    masks = Masks(info)
    count = counts[1:2, :]
    params = [norm_of(got, info, batch, chan, k, 0, masks.local_out, count) for k in range(chan)]
    store_norms(norms, params)
    chunks = z.shape[0] // CHUNK

    def store(t, lanes, value):
        a[at(t, CHUNK), lanes] = flat(value).astype(BF)

    activate_into(near, params, tabs, 1, chan, info, masks, chunks, store)
    a.send()
    z[...] = dot(a[...], w.use()[...])
    rows = wide_sums(z, zc, chunks, masks)
    broadcast_rows(stats, rows)


def wide_sums(z, zc, chunks, masks):
    blocks = z.shape[1] // LANES
    totals, squares = [], []
    for q in range(blocks):
        lanes = slice(q * LANES, (q + 1) * LANES)
        total, square = sums_of(z, chunks, lanes)
        totals.append(total)
        squares.append(square)
        if zc is not None:
            centre_into(zc, z, chunks, lanes, total / masks.local_out)
    return totals + squares


def wide_norm(got, info, batch, chan, k, row, blocks, local, count):
    column = info[0] ^ k
    total = got[column]
    for n in range(1, batch):
        total = total + got[n * chan + column]
    mine = got[info[1] * chan + column]
    mean = total[row : row + blocks] / count
    inverse = lax.rsqrt(total[row + blocks : row + 2 * blocks] / count - mean * mean + EPS)
    return mine[row : row + blocks] / local - mean, inverse


def merge_act_kernel(batch, chan, pair, info, got3, got2, *refs):
    size = len(pair)
    near3, nears = refs[:size], refs[size : 2 * size]
    tabs, counts, *outs, own, norms = refs[2 * size :]
    nears, got2 = ready(nears), ready(got2)
    masks = Masks(info)
    count = counts[1:2, :]
    rows, width = near3[0].shape
    blocks = width // LANES
    lines = []
    for k in pair:
        one = wide_norm(got3, info, batch, chan, k, 0, blocks, masks.local_out, count)
        two = wide_norm(got2, info, batch, chan, k, 8, blocks, masks.local_out, count)
        if k == 0:
            for n, value in enumerate(one + two):
                norms[n * blocks : (n + 1) * blocks, :] = value
        gain, bias = 8, 8 + 3 * blocks
        scale3 = one[1] * tabs[k, gain : gain + blocks, :]
        scales = two[1] * tabs[k, gain + blocks : gain + 2 * blocks, :]
        shift = (
            one[0] * scale3
            + two[0] * scales
            + tabs[k, bias : bias + blocks, :]
            + tabs[k, bias + blocks : bias + 2 * blocks, :]
        )
        lines.append((scale3, scales, shift))

    def step(t, _):
        mask = masks.small(t)
        for n, k in enumerate(pair):
            scale3, scales, shift = lines[n]
            for q in range(blocks):
                lanes = slice(q * LANES, (q + 1) * LANES)
                pre = (
                    cube(near3[n][at(t, CHUNK), lanes]) * scale3[q : q + 1]
                    + cube(nears[n][at(t, CHUNK), lanes]) * scales[q : q + 1]
                    + shift[q : q + 1]
                )
                value = flat(keep(mask, gelu(pre)))
                if k == 0:
                    own[at(t, CHUNK), lanes] = value
                outs[n][at(t, CHUNK), lanes] = value.astype(BF)
        return 0

    lax.fori_loop(0, rows // CHUNK, step, 0)


def contract_kernel(chan, w, info, *refs):
    y, (zc, stats, z) = refs[:chan], refs[chan:]
    masks = Masks(info)
    rows, width = y[0].shape
    chunks = rows // CHUNK
    w = w.use()
    total = None
    for k in range(chan):
        term = dot(y[k][...], w[at(info[0] ^ k, width), :])
        total = term if total is None else total + term
    z[...] = total
    total, squares = sums_of(z, chunks, slice(0, LANES))
    broadcast_rows(stats, (total, squares))
    centre_into(zc, z, chunks, slice(0, LANES), total / masks.local_out)


def spatial_kernel(batch, chan, w, info, got, *refs):
    near, (tabs, counts, a, zc, stats, norms, held, z) = refs[:chan], refs[chan:]
    masks = Masks(info)
    count = counts[1:2, :]
    params = [norm_of(got, info, batch, chan, k, 0, masks.local_out, count) for k in range(chan)]
    store_norms(norms, params)
    rows, width = a.shape
    chunks = rows // CHUNK
    for tap in range(3):
        held[tap, 0:CHUNK, :] = jnp.zeros((CHUNK, width), BF)
        held[tap, rows + CHUNK : rows + 2 * CHUNK, :] = jnp.zeros((CHUNK, width), BF)

    def store(t, lanes, value):
        plain = flat(value).astype(BF)
        a[at(t, CHUNK), lanes] = plain
        held[1, at(t + 1, CHUNK), lanes] = plain
        held[0, at(t + 1, CHUNK), lanes] = flat(push_right(value)).astype(BF)
        held[2, at(t + 1, CHUNK), lanes] = flat(push_left(value)).astype(BF)

    activate_into(near, params, tabs, 2, chan, info, masks, chunks, store)
    a.send()
    acc = None
    w = w.use()
    for i in range(3):
        for j in range(3):
            term = dot(held[j, i * CHUNK : i * CHUNK + rows, :], w[i, j])
            acc = term if acc is None else acc + term
    z[...] = acc
    total, squares = sums_of(z, chunks, slice(0, LANES), masks.small)
    broadcast_rows(stats, (total, squares))
    centre_into(zc, z, chunks, slice(0, LANES), total / masks.local_out)


def last_kernel(batch, chan, w, info, got, *refs):
    near, (tabs, counts, a, z, stats, norms) = refs[:chan], refs[chan:]
    masks = Masks(info)
    count = counts[1:2, :]
    params = [norm_of(got, info, batch, chan, k, 0, masks.local_out, count) for k in range(chan)]
    store_norms(norms, params)
    chunks = a.shape[0] // CHUNK

    def store(t, lanes, value):
        a[at(t, CHUNK), lanes] = flat(value).astype(BF)

    activate_into(near, params, tabs, 3, chan, info, masks, chunks, store)
    a.send()
    z[...] = dot(a[...], w.use()[...])
    broadcast_rows(stats, wide_sums(z, None, chunks, masks))


def output_kernel(info, got, z, own, loss, tabs, counts, result, g, stats, norms):
    masks = Masks(info)
    own, loss = ready(own), ready(loss)
    count = counts[1:2, :]
    total = whole(got)
    rows, width = z.shape
    blocks = width // LANES
    chunks = rows // CHUNK
    mean = total[0:blocks] / count
    inverse = lax.rsqrt(total[blocks : 2 * blocks] / count - mean * mean + EPS)
    norms[0:blocks, :] = mean
    norms[blocks : 2 * blocks, :] = inverse
    gain = tabs[0, 8 + 2 * blocks : 8 + 3 * blocks, :]
    bias = tabs[0, 8 + 5 * blocks : 8 + 6 * blocks, :]
    small = result.shape[1]

    def step(t, carry):
        mask = masks.small(t)
        sums = []
        for q in range(blocks):
            lanes = slice(q * LANES, (q + 1) * LANES)
            zhat = (cube(z[at(t, CHUNK), lanes]) - mean[q : q + 1]) * inverse[q : q + 1]
            pre = zhat * gain[q : q + 1] + bias[q : q + 1] + cube(own[at(t, CHUNK), lanes])
            result[t, :, :, lanes] = keep(mask, gelu(pre))[:small].astype(BF)
            u = keep(mask, gelu_slope(pre)) * padded(loss[t, :, :, lanes].astype(F32))
            g[at(t, CHUNK), lanes] = flat(u)
            sums.append((carry[q][0] + total_of(u * zhat), carry[q][1] + total_of(u)))
        return tuple(sums)

    zero = jnp.zeros((IMAGES, LANES), F32)
    sums = lax.fori_loop(0, chunks, step, ((zero, zero),) * blocks)
    broadcast_rows(stats, [row_sum(s[0]) for s in sums] + [row_sum(s[1]) for s in sums])


def share_stage(da, near, norms, tabs, gain, chan, batch, info, masks, chunks, pieces, stats):
    zero = jnp.zeros((IMAGES, LANES), F32)
    for k in range(chan):
        lanes = lane_block(info[0] ^ k)
        offset, inverse = norms[2 * k : 2 * k + 1, :], norms[2 * k + 1 : 2 * k + 2, :]
        scale, bias = tabs[k, gain : gain + 1, :], tabs[k, gain + 4 : gain + 5, :]

        def step(t, carry, k=k, lanes=lanes, offset=offset, inverse=inverse, scale=scale, bias=bias):
            share = da[at(t, CHUNK), lanes]
            zhat = (cube(near[k][at(t, CHUNK), :]) + offset) * inverse
            u = keep(masks.small(t), gelu_slope(zhat * scale + bias)) * cube(share)
            pieces[k][at(t, CHUNK), :] = share.astype(pieces[k].dtype)
            return carry[0] + total_of(u * zhat), carry[1] + total_of(u)

        first, second = lax.fori_loop(0, chunks, step, (zero, zero))
        block = jnp.concatenate(
            [row_sum(first), row_sum(second), jnp.zeros((stats.shape[1] - 2, LANES), F32)], axis=0
        )
        for n in range(batch):
            stats[n * chan + (info[0] ^ k)] = block


def own_stage(got, parts, near, norms, tabs, gain, count, masks, chunks, sums, store):
    total = whole(got)
    gg, gb = total[0:1], total[1:2]
    fill_rows(sums, (gg, gb))
    offset, inverse = norms[0:1, :], norms[1:2, :]
    scale, bias = tabs[0, gain : gain + 1, :], tabs[0, gain + 4 : gain + 5, :]
    per_cell, per_hat = gb / count, gg / count
    front = scale * inverse

    def step(t, _):
        mask = masks.small(t)
        da = cube(parts[0][at(t, CHUNK), :])
        for part in parts[1:]:
            da = da + cube(part[at(t, CHUNK), :])
        zhat = (cube(near[at(t, CHUNK), :]) + offset) * inverse
        u = gelu_slope(zhat * scale + bias) * da
        store(t, keep(mask, front * (u - (per_cell + zhat * per_hat))))
        return 0

    lax.fori_loop(0, chunks, step, 0)


def back_last_kernel(batch, chan, w, info, got, g, z, norms6, tabs, counts, *refs):
    near, (norms, dz, *pieces, stats, sums, da) = refs[:chan], refs[chan:]
    masks = Masks(info)
    z = ready(z)
    count = counts[1:2, :]
    total = whole(got)
    rows, width = z.shape
    blocks = width // LANES
    chunks = rows // CHUNK
    gg, gb = total[0:blocks] / count, total[blocks : 2 * blocks] / count
    sums[...] = total
    mean, inverse = norms6[0:blocks, :], norms6[blocks : 2 * blocks, :]
    front = tabs[0, 8 + 2 * blocks : 8 + 3 * blocks, :] * inverse

    def step(t, _):
        mask = masks.small(t)
        for q in range(blocks):
            lanes = slice(q * LANES, (q + 1) * LANES)
            zhat = (cube(z[at(t, CHUNK), lanes]) - mean[q : q + 1]) * inverse[q : q + 1]
            value = cube(g[at(t, CHUNK), lanes]) - (gb[q : q + 1] + zhat * gg[q : q + 1])
            dz[at(t, CHUNK), lanes] = flat(keep(mask, front[q : q + 1] * value)).astype(BF)
        return 0

    lax.fori_loop(0, chunks, step, 0)
    dz.send()
    da[...] = dot(dz[...], w.use()[...], ((1,), (1,)))
    near = ready(near)
    share_stage(da, near, norms, tabs, 3, chan, batch, info, masks, chunks, pieces, stats)


def back_spatial_kernel(batch, chan, w, info, got, *refs):
    parts, refs = refs[:chan], refs[chan:]
    own, norms5, tabs, counts = refs[:4]
    near, (norms, spread, *pieces, stats, sums, held, da) = refs[4 : 4 + chan], refs[4 + chan :]
    masks = Masks(info)
    own = ready(own)
    rows = own.shape[0]
    chunks = rows // CHUNK
    for tap in range(3):
        held[tap, 0:CHUNK, :] = jnp.zeros((CHUNK, LANES), BF)
        held[tap, rows + CHUNK : rows + 2 * CHUNK, :] = jnp.zeros((CHUNK, LANES), BF)

    def store(t, value):
        held[1, at(t + 1, CHUNK), :] = flat(value).astype(BF)
        held[0, at(t + 1, CHUNK), :] = flat(push_left(value)).astype(BF)
        held[2, at(t + 1, CHUNK), :] = flat(push_right(value)).astype(BF)

    own_stage(got, parts, own, norms5, tabs, 3, counts[1:2, :], masks, chunks, sums, store)
    acc = None
    w = w.use()
    for i in range(3):
        for j in range(3):
            value = held[j, (2 - i) * CHUNK : (2 - i) * CHUNK + rows, :]
            spread[:, (3 * i + j) * LANES : (3 * i + j + 1) * LANES] = value
            term = dot(value, w[i, j], ((1,), (1,)))
            acc = term if acc is None else acc + term
    da[...] = acc
    near = ready(near)
    share_stage(da, near, norms, tabs, 2, chan, batch, info, masks, chunks, pieces, stats)


def back_contract_kernel(info, got, *refs):
    *parts, own, norms, tabs, counts, dz, sums, copy = refs
    own = ready(own)
    masks = Masks(info)

    def store(t, value):
        plain = flat(value).astype(BF)
        dz[at(t, CHUNK), :] = plain
        copy[at(t, CHUNK), :] = plain

    own_stage(got, parts, own, norms, tabs, 2, counts[1:2, :], masks, own.shape[0] // CHUNK, sums, store)


def back_merge_kernel(chan, info, *refs):
    dz, w = refs[:chan], refs[chan : 2 * chan]
    g, near3, nears, norms, tabs, g1, stats, dy = refs[2 * chan :]
    masks = Masks(info)
    rows, width = dy.shape
    blocks = width // LANES
    chunks = rows // CHUNK
    acc = None
    for k in range(chan):
        term = dot(dz[k][...], ready(w[k])[...], ((1,), (1,)))
        acc = term if acc is None else acc + term
    dy[...] = acc
    g, near3, nears = ready(g), ready(near3), ready(nears)
    zero = jnp.zeros((IMAGES, LANES), F32)
    lines = [[], [], []]
    for q in range(blocks):
        lanes = slice(q * LANES, (q + 1) * LANES)
        off3, inv3, offs, invs = (norms[n * blocks + q : n * blocks + q + 1, :] for n in range(4))
        gain, bias = 8, 8 + 3 * blocks
        gain3, gains = tabs[0, gain + q : gain + q + 1, :], tabs[0, gain + blocks + q : gain + blocks + q + 1, :]
        shift = tabs[0, bias + q : bias + q + 1, :] + tabs[0, bias + blocks + q : bias + blocks + q + 1, :]

        def step(t, carry):
            zhat3 = (cube(near3[at(t, CHUNK), lanes]) + off3) * inv3
            zhats = (cube(nears[at(t, CHUNK), lanes]) + offs) * invs
            pre = zhat3 * gain3 + zhats * gains + shift
            up = cube(g[at(t, CHUNK), lanes]) + cube(dy[at(t, CHUNK), lanes])
            u = keep(masks.small(t), gelu_slope(pre)) * up
            g1[at(t, CHUNK), lanes] = flat(u)
            return (
                carry[0] + total_of(u * zhat3),
                carry[1] + total_of(u * zhats),
                carry[2] + total_of(u),
            )

        done = lax.fori_loop(0, chunks, step, (zero, zero, zero))
        for n in range(3):
            lines[n].append(row_sum(done[n]))
    broadcast_rows(stats, lines[0] + lines[1] + lines[2])


def back_enlarge_kernel(batch, chan, w, info, got, g1, near3, nears, norms3, tabs, counts, *refs):
    near, (norms, dz3, dzs, *pieces, stats, sums, da) = refs[:chan], refs[chan:]
    masks = Masks(info)
    near3, nears = ready(near3), ready(nears)
    count = counts[1:2, :]
    total = whole(got)
    sums[...] = total
    rows, width = g1.shape
    blocks = width // LANES
    chunks = rows // CHUNK
    total = total / count
    gg3, ggs, gb = (total[n * blocks : (n + 1) * blocks] for n in range(3))
    off3, inv3, offs, invs = (norms3[n * blocks : (n + 1) * blocks, :] for n in range(4))
    front3 = tabs[0, 8 : 8 + blocks, :] * inv3
    fronts = tabs[0, 8 + blocks : 8 + 2 * blocks, :] * invs

    def step(t, _):
        mask = masks.small(t)
        for q in range(blocks):
            lanes = slice(q * LANES, (q + 1) * LANES)
            line = slice(q, q + 1)
            u = cube(g1[at(t, CHUNK), lanes]) - gb[line]
            zhat3 = (cube(near3[at(t, CHUNK), lanes]) + off3[line]) * inv3[line]
            zhats = (cube(nears[at(t, CHUNK), lanes]) + offs[line]) * invs[line]
            dz3[at(t, CHUNK), lanes] = flat(keep(mask, front3[line] * (u - zhat3 * gg3[line]))).astype(BF)
            dzs[at(t, CHUNK), lanes] = flat(keep(mask, fronts[line] * (u - zhats * ggs[line]))).astype(BF)
        return 0

    lax.fori_loop(0, chunks, step, 0)
    da[...] = dot(dz3[...], w.use()[...], ((1,), (1,)))
    near = ready(near)
    share_stage(da, near, norms, tabs, 1, chan, batch, info, masks, chunks, pieces, stats)


def back_strided_kernel(info, got, *refs):
    *parts, own, norms, tabs, counts, dz, moved, sums, held = refs
    masks = Masks(info)
    own = ready(own)
    rows = own.shape[0]
    for tap in range(2):
        held[tap, rows : rows + CHUNK, :] = jnp.zeros((CHUNK, LANES), BF)

    def store(t, value):
        plain = flat(value).astype(BF)
        dz[at(t, CHUNK), :] = plain
        held[0, at(t, CHUNK), :] = plain
        held[1, at(t, CHUNK), :] = flat(push_left(value)).astype(BF)

    own_stage(got, parts, own, norms, tabs, 1, counts[1:2, :], masks, rows // CHUNK, sums, store)
    for down in range(2):
        for right in range(2):
            n = 2 * down + right
            moved[:, n * LANES : (n + 1) * LANES] = held[right, down * CHUNK : down * CHUNK + rows, :]


TAPS = {0: ((1, 0),), 1: ((2, 0), (0, 1))}


def back_first_kernel(chan, info, *refs):
    dz, w = refs[:chan], refs[chan : 2 * chan]
    near, norms, tabs, u_out, stats, held, joined, da = refs[2 * chan :]
    masks = Masks(info)
    rows = dz[0].shape[0]
    chunks = rows // CHUNK
    for tap in range(2):
        held[tap, rows : rows + CHUNK, :] = jnp.zeros((CHUNK, chan * LANES), BF)
    for k in range(chan):
        joined[:, :, :, k * LANES : (k + 1) * LANES] = ready(w[k])[...]
    near = ready(near)

    def shift(t, _):
        for k in range(chan):
            lanes = slice(k * LANES, (k + 1) * LANES)
            value = dz[k][at(t, CHUNK), :]
            held[0, at(t, CHUNK), lanes] = value
            held[1, at(t, CHUNK), lanes] = flat(push_left(cube(value))).astype(BF)
        return 0

    lax.fori_loop(0, chunks, shift, 0)
    offset, inverse = norms[0:1, :], norms[1:2, :]
    scale, bias = tabs[0, 0:1, :], tabs[0, 4:5, :]
    zero = jnp.zeros((IMAGES, LANES), F32)
    sums = (zero, zero)
    for p in range(2):
        for q in range(2):
            acc = None
            for a, down in TAPS[p]:
                for b, right in TAPS[q]:
                    term = dot(
                        held[right, down * CHUNK : down * CHUNK + rows, :], joined[a, b], ((1,), (1,))
                    )
                    acc = term if acc is None else acc + term
            da[q] = acc

        def step(t, carry, p=p):
            r = 2 * t + p
            place = at(r, LINE)
            zhat = (cube(near[place, :]) + offset) * inverse
            up = merged(cube(da[0, at(t, CHUNK), :]), cube(da[1, at(t, CHUNK), :]))
            u = keep(masks.large(r), gelu_slope(zhat * scale + bias)) * up
            u_out[place, :] = flat(u)
            return carry[0] + total_of(u * zhat), carry[1] + total_of(u)

        sums = lax.fori_loop(0, chunks, step, sums)
    broadcast_rows(stats, (row_sum(sums[0]), row_sum(sums[1])))


def back_first_own_kernel(info, got, u, near, norms, tabs, counts, dz, sums, copy):
    masks = Masks(info)
    count = counts[0:1, :]
    total = whole(got)
    gg, gb = total[0:1], total[1:2]
    fill_rows(sums, (gg, gb))
    per_cell, per_hat = gb / count, gg / count
    near = ready(near)
    offset, inverse = norms[0:1, :], norms[1:2, :]
    front = tabs[0, 0:1, :] * inverse

    def step(r, _):
        place = at(r, LINE)
        zhat = (cube(near[place, :]) + offset) * inverse
        value = front * (cube(u[place, :]) - (per_cell + zhat * per_hat))
        plain = flat(keep(masks.large(r), value)).astype(BF)
        dz[place, :] = plain
        copy[place, :] = plain
        return 0

    lax.fori_loop(0, SIDE, step, 0)


def leave_kernel(chan, info, *refs):
    dz, dzs = refs[:chan], refs[chan : 2 * chan]
    w, ws = refs[2 * chan : 3 * chan], refs[3 * chan : 4 * chan]
    out, dm, extra = refs[4 * chan :]
    masks = Masks(info)
    acc = None
    for k in range(chan):
        term = dot(ready(dzs[k])[...], ready(ws[k])[...], ((1,), (1,)))
        acc = term if acc is None else acc + term
    extra[...] = acc
    width = out.shape[3]
    part = 2 * LINE
    w = ready(w)

    def product(t, _):
        total = None
        for k in range(chan):
            term = dot(dz[k][at(t, part), :], w[k][...], ((1,), (1,)))
            total = term if total is None else total + term
        dm[at(t, part), :] = total
        return 0

    lax.fori_loop(0, dm.shape[0] // part, product, 0)

    def step(i, _):
        for p in range(2):
            r = 2 * i + p
            mask = masks.large(r)
            for q in range(width // LANES):
                lanes = slice(q * LANES, (q + 1) * LANES)
                value = cube(dm[at(r, LINE), lanes])
                if p == 0:
                    more = cube(extra[at(i, CHUNK), lanes])
                    value = value + merged(more, jnp.zeros_like(more))
                out[r, :, :, lanes] = keep(mask, value).astype(BF)
        return 0

    lax.fori_loop(0, SIDE // 2, step, 0)


def radices_of(batch):
    sizes, units, unit = [], [], 1
    while unit < batch:
        size = 2 if not sizes or batch // unit == 2 else 4
        sizes.append(size)
        units.append(unit)
        unit *= size
    return sizes, units


def numbers_of(sizes, units):
    numbers = [0]
    for size, unit in reversed(list(zip(sizes, units))):
        numbers = [r + m * unit for m in range(size) for r in numbers]
    return numbers


def early_products(chan, info, ins, outs):
    outs[0][...] = dot(ins[0][...], ins[1][...], ((0,), (0,)))
    outs[1][...] = dot(ins[2][...], ins[3][...], ((0,), (0,)))


def rows_products(chan, info, ins, outs):
    *pieces, right = ins
    size = pieces[0].shape[1]
    for k, piece in enumerate(pieces):
        outs[0][at(info[0] ^ k, size), :] = dot(piece[...], right[...], ((0,), (0,)))


def wide_products(chan, info, ins, outs):
    a2, dz3, even, dzs = ins
    outs[0][...] = dot(a2[...], dz3[...], ((0,), (0,)))
    outs[1][...] = dot(even[...], dzs[...], ((0,), (0,)))


def strided_products(chan, info, ins, outs):
    a1, moved = ins
    rows = moved.shape[0]
    for p in range(2):
        for q in range(2):
            start = CHUNK if p else 0
            plane = a1[1 + q, 1 - p, start : start + rows, :]
            for a, down in TAPS[p]:
                for b, right in TAPS[q]:
                    n = 2 * down + right
                    tap = 3 * a + b
                    outs[0][:, tap * LANES : (tap + 1) * LANES] = dot(
                        plane, moved[:, n * LANES : (n + 1) * LANES], ((0,), (0,))
                    )


def cut_product(ref, number, batch):
    rows = ref.shape[0] // batch
    size = MID // batch
    for n in range(rows // size):
        for lane in range(0, ref.shape[1], LANES):
            first = number * rows + n * size
            yield ref[pl.ds(pl.multiple_of(first, size), size), lane : lane + LANES]


def place_chunk(blocks, outs, layout, number):
    blocks = list(blocks)
    for out, (taps, repeats) in zip(outs, layout):
        size = blocks[0].shape[0]
        for n in range(taps * repeats):
            for lane in range(0, out.shape[-1], LANES):
                value = blocks.pop(0).astype(F32)
                if taps > 1:
                    out[n, at(number, size), lane : lane + LANES] = value
                else:
                    first = (number * repeats + n) * size
                    out[pl.ds(pl.multiple_of(first, size), size), lane : lane + LANES] = value


def slot_kernel(batch, chan, plan, info, *refs):
    ins, outs = refs[: plan["ins"]], refs[plan["ins"] :]
    for job in plan["jobs"]:
        if job["kind"] == "pack":
            products = [outs[n] for n in job["products"]]
            job["compute"](chan, info, ready([ins[n] for n in job["ins"]]), products)
            for place, r in enumerate(job["numbers"]):
                number = info[1] ^ r
                blocks = [v for ref in products for v in cut_product(ref, number, batch)]
                for n, block in enumerate(blocks):
                    put(outs, job["targets"], place * len(blocks) + n, block.astype(BF))
        else:
            sources = [(ready(ins[n]), first) for n, first in job["sources"]]
            size = job.get("size")
            if job["kind"] == "fold":
                for n in range(size):
                    total = None
                    for ref, first in sources:
                        value = ref[first + n].astype(F32)
                        total = value if total is None else total + value
                    put(outs, job["targets"], n, total.astype(BF))
            elif job["kind"] == "join":
                for m, (ref, first) in enumerate(sources):
                    for n in range(size):
                        put(outs, job["targets"], m * size + n, ref[first + n])
            else:
                width = job["width"]
                finals = [outs[n] for n in job["finals"]]
                for (ref, first), numbers in zip(sources, job["numbers"]):
                    for place, r in enumerate(numbers):
                        start = first + place * width
                        place_chunk(
                            [ref[start + n] for n in range(width)], finals, job["layout"], info[1] ^ r
                        )


def put(outs, targets, n, block):
    for out, place, first, count in targets:
        if first <= n < first + count:
            outs[out][place + n - first] = block


def solution(mesh):
    batch = mesh.shape["batch"]
    chan = mesh.shape["chan"]
    everyone = ("batch", "chan")
    devices = batch * chan
    half = chan // 2
    pair = (0, half)

    def swap(v, mask, axis="chan"):
        return lax.ppermute(v, axis, [(k, k ^ mask) for k in range(mesh.shape[axis])])

    def widen(found):
        found = dict(found)
        mask = half // 2
        while mask:
            for k in list(found):
                found[k ^ mask] = swap(found[k], mask)
            mask //= 2
        return [found[k] for k in range(chan)]

    def gather(v):
        return widen({0: v, half: swap(v, half)})

    def gather_direct(v):
        return [v] + [swap(v, k) for k in range(1, chan)]

    def deliver(pieces):
        return [pieces[0]] + [swap(pieces[k], k) for k in range(1, chan)]

    def exchange(stats):
        return lax.all_to_all(stats, everyone, 0, 0)

    def exchange_batch(stats):
        return lax.all_to_all(stats, "batch", 0, 0)

    def cut(v, axis):
        size = v.shape[axis] // chan
        me = lax.axis_index("chan")
        return [lax.dynamic_slice_in_dim(v, (me ^ k) * size, size, axis) for k in range(chan)]

    sizes, units = radices_of(batch)
    levels = len(sizes)

    class Gradient:
        def __init__(self, compute, ins, products, layout, shapes):
            self.compute, self.ins, self.products = compute, ins, products
            self.layout, self.shapes = layout, shapes
            self.width = sum(math.prod(v) for v in products) // (MID * LANES)
            self.started = 0
            self.result = None

        def partners(self, step):
            level = step if step < levels else 2 * levels - 1 - step
            return [m * units[level] for m in range(1, sizes[level])]

    def slot(info, gradients, last):
        ins, outs, scratch, jobs = [], [], [], []
        bundles = {}
        received = [v for g in gradients if g.started for v, _ in g.got]
        size = MID // batch

        def give(array):
            for n, v in enumerate(ins):
                if v is array:
                    return n
            ins.append(array)
            return len(ins) - 1

        for g in gradients:
            job = {"targets": []}
            if not g.started:
                job.update(kind="pack", compute=g.compute, numbers=numbers_of(sizes, units))
                job["ins"] = [give(v) for v in g.ins]
                total = batch * g.width
            else:
                done = g.started - 1
                sources = [(give(g.kept), 0)] + [(give(v), first) for v, first in g.got]
                if done < levels:
                    total = g.amount
                    job.update(kind="fold", sources=sources, size=total)
                elif g.started < 2 * levels:
                    total = g.amount * len(sources)
                    job.update(kind="join", sources=sources, size=g.amount)
                    masks = [0] + g.partners(done)
                    g.numbers = [r ^ m for m in masks for r in g.numbers]
                else:
                    masks = [0] + g.partners(done)
                    job.update(kind="place", sources=sources, layout=g.layout, width=g.width)
                    job["numbers"] = [[r ^ m for r in g.numbers] for m in masks]
                    job["finals"] = g
                    jobs.append((g, job, None))
                    continue
            jobs.append((g, job, total))
        for g, job, total in jobs:
            if total is None:
                job["finals"] = list(range(len(outs), len(outs) + len(g.shapes)))
                outs += [(v, F32, "far") for v in g.shapes]
                continue
            step = g.started
            masks = g.partners(step)
            if step < levels:
                share = total // (len(masks) + 1)
                firsts = [share * m for m in range(len(masks) + 1)]
            else:
                share = total
                firsts = [0] * (len(masks) + 1)
                if step == levels:
                    g.numbers = [0]
            g.amount = share
            job["targets"].append((len(outs), 0, firsts[0], share))
            g.kept = len(outs)
            outs.append(((share, size, LANES), BF, "far"))
            g.next = []
            for mask, first in zip(masks, firsts[1:]):
                place = bundles.get(mask, 0)
                g.next.append((mask, place))
                bundles[mask] = place + share
                job["targets"].append((mask, place, first, share))
        order = sorted(bundles)
        where = {mask: len(outs) + n for n, mask in enumerate(order)}
        outs += [((bundles[mask], size, LANES), BF, "far") for mask in order]
        for g, job, total in jobs:
            if total is not None:
                job["targets"] = [job["targets"][0]] + [(where[v[0]], *v[1:]) for v in job["targets"][1:]]
            if job["kind"] == "pack":
                job["products"] = list(range(len(outs) + len(scratch), len(outs) + len(scratch) + len(g.products)))
                scratch += [(v, F32) for v in g.products]
        plan = {"ins": len(ins), "jobs": [job for _, job, _ in jobs]}
        given = [v if any(v is w for w in received) else far(v) for v in ins]
        made = in_vmem(
            functools.partial(slot_kernel, batch, chan, plan), [info, *given], outs, scratch, after=[last]
        )
        moved = {mask: swap(made[where[mask]], mask, "batch") for mask in order}
        for g, job, total in jobs:
            if total is None:
                g.result = [made[n] for n in job["finals"]]
            else:
                g.kept = made[g.kept]
                g.got = [(moved[mask], place) for mask, place in g.next]
                g.started += 1
        return made[0]

    def local(
        entry_activation,
        image_bounds,
        loss_sensitivity,
        first_contract_kernel,
        first_strided_kernel,
        first_enlarge_kernel,
        projection_kernel,
        second_contract_kernel,
        second_spatial_kernel,
        second_enlarge_kernel,
        bottleneck_gains,
        bottleneck_biases,
        wide_gain_vector,
        wide_bias_vector,
    ):
        images, side, _, quarter = entry_activation.shape
        small = side // 2
        wide = first_enlarge_kernel.shape[1]
        blocks = wide // LANES
        rows, large = small * CHUNK, side * LINE
        depth = quarter * chan
        mid = first_contract_kernel.shape[1] * chan
        assert mid == MID and images == IMAGES and side == SIDE
        piece, full, line = ((rows, LANES), BF), ((rows, wide), BF), ((large, LANES), BF)
        f32s = lambda *shape: (shape, F32)

        info = jnp.concatenate(
            [lax.axis_index("chan")[None], lax.axis_index("batch")[None], image_bounds.T.reshape(-1)]
        ).astype(jnp.int32)
        (own,) = in_vmem(
            enter_kernel, [info, entry_activation.transpose(1, 2, 0, 3)], [((large, quarter), BF)]
        )
        source = gather(own)
        table = jnp.concatenate(
            [
                bottleneck_gains,
                bottleneck_biases,
                wide_gain_vector.reshape(-1, LANES),
                wide_bias_vector.reshape(-1, LANES),
            ]
        )
        tabs = jnp.stack(gather_direct(table))
        loss = loss_sensitivity.transpose(1, 2, 0, 3)

        z1, stats1 = in_vmem(
            functools.partial(first_kernel, chan),
            [far(first_contract_kernel), info, *source],
            [line, f32s(devices, 8, LANES)],
            [f32s(large, LANES)],
        )
        got1 = exchange(stats1)
        z1_far = swap(z1, pair[1])
        even, zs, stats_s, *source_far = in_vmem(
            functools.partial(shortcut_kernel, chan),
            [far(projection_kernel), info, *source],
            [((rows, depth), BF, "far"), (*full, "far"), f32s(2 * blocks, LANES)],
            [f32s(rows, wide)],
            save=range(2, 2 + chan),
        )
        zs_far = swap(zs, pair[1])
        *acts, norms1, counts, z1 = in_vmem(
            functools.partial(first_act_kernel, batch, chan, pair),
            [info, got1, z1, z1_far, tabs],
            [line, line, f32s(8, LANES), f32s(8, LANES)],
            after=[zs],
            save=[2],
        )
        acts = widen(dict(zip(pair, acts)))
        a1, z2, stats2 = in_vmem(
            functools.partial(strided_kernel, chan),
            [far(first_strided_kernel), info, *acts, stats_s],
            [((3, 2, rows + CHUNK, mid), BF, "far"), piece, f32s(devices, 16, LANES)],
            [f32s(rows, LANES)],
        )
        got2 = exchange(stats2)
        near2 = gather_direct(z2)
        a2, z3, stats3, norms2, got2, *near2 = in_vmem(
            functools.partial(enlarge_kernel, batch, chan),
            [far(first_enlarge_kernel), info, got2, *near2, tabs, counts],
            [((rows, mid), BF, "far"), full, f32s(devices, 2 * blocks, LANES), f32s(2 * chan, LANES)],
            [f32s(rows, wide)],
            save=range(2, 3 + chan),
        )
        got3 = exchange(stats3)
        z3_far = swap(z3, pair[1])
        *y1, y1_own, norms3, z3 = in_vmem(
            functools.partial(merge_act_kernel, batch, chan, pair),
            [info, got3, far(got2), z3, z3_far, far(zs), far(zs_far), tabs, counts],
            [full, full, ((rows, wide), F32, "far"), f32s(4 * blocks, LANES)],
            save=[3],
        )
        y1 = widen(dict(zip(pair, y1)))
        z4, stats4, *y1 = in_vmem(
            functools.partial(contract_kernel, chan),
            [far(second_contract_kernel), info, *y1],
            [piece, f32s(devices, 8, LANES)],
            [f32s(rows, LANES)],
            save=range(2, 2 + chan),
        )

        got4 = exchange(stats4)
        near4 = gather_direct(z4)
        a4, z5, stats5, norms4, *near4 = in_vmem(
            functools.partial(spatial_kernel, batch, chan),
            [far(second_spatial_kernel), info, got4, *near4, tabs, counts],
            [((rows, mid), BF, "far"), piece, f32s(devices, 8, LANES), f32s(2 * chan, LANES)],
            [((3, rows + 2 * CHUNK, mid), BF), f32s(rows, LANES)],
            save=range(3, 3 + chan),
        )
        got5 = exchange(stats5)
        near5 = gather_direct(z5)
        a5, z6, stats6, norms5, *near5 = in_vmem(
            functools.partial(last_kernel, batch, chan),
            [far(second_enlarge_kernel), info, got5, *near5, tabs, counts],
            [
                ((rows, mid), BF, "far"),
                f32s(rows, wide),
                f32s(batch, 2 * blocks, LANES),
                f32s(2 * chan, LANES),
            ],
            save=range(3, 3 + chan),
        )
        got6 = exchange_batch(stats6)
        w1t = deliver(cut(first_contract_kernel, 0))
        w2t = deliver(cut(first_strided_kernel, 2))
        wpt = deliver(cut(projection_kernel, 0))
        w4t = deliver(cut(second_contract_kernel, 0))
        result, g2, stats7, norms6, z6 = in_vmem(
            output_kernel,
            [info, got6, z6, far(y1_own), far(loss), tabs, counts],
            [
                ((small, small, images, wide), BF, "far"),
                f32s(rows, wide),
                f32s(batch, 2 * blocks, LANES),
                f32s(2 * blocks, LANES),
            ],
            save=[2],
        )

        shares = [f32s(rows, LANES)] + [piece] * (chan - 1)
        routed = f32s(devices, 8, LANES)
        tap_lanes = 9 * LANES
        got7 = exchange_batch(stats7)
        dz6, *sent, stats8, sums6, g2 = in_vmem(
            functools.partial(back_last_kernel, batch, chan),
            [far(second_enlarge_kernel), info, got7, g2, far(z6), norms6, tabs, counts, *fars(near5), norms5],
            [(*full, "far"), *shares, routed, f32s(2 * blocks, LANES)],
            [f32s(rows, mid)],
            after=[*w2t, *w1t, *w4t],
            save=[3],
        )
        got8 = exchange(stats8)
        parts = deliver(sent)
        spread5, *sent, stats9, sums5 = in_vmem(
            functools.partial(back_spatial_kernel, batch, chan),
            [
                far(second_spatial_kernel), info, got8, *parts, far(near5[0]), norms5, tabs, counts,
                *fars(near4), norms4,
            ],
            [((rows, tap_lanes), BF, "far"), *shares, routed, f32s(8, LANES)],
            [((3, rows + 2 * CHUNK, LANES), BF), f32s(rows, mid)],
            after=[*wpt],
        )
        got9 = exchange(stats9)
        parts = deliver(sent)
        early = Gradient(
            early_products,
            [a5, dz6, a4, spread5],
            [(mid, wide), (mid, tap_lanes)],
            ((1, 1), (9, 1)),
            [(mid, wide), (9, mid, LANES)],
        )
        last = slot(info, [early], sums5)
        dz4, sums4, dz4_far = in_vmem(
            back_contract_kernel,
            [info, got9, *parts, far(near4[0]), norms4, tabs, counts],
            [piece, f32s(8, LANES), (*piece, "far")],
            after=[last],
        )
        dz4_all = gather_direct(dz4)
        narrowing = Gradient(
            rows_products, [*y1, dz4_far], [(wide * chan, LANES)], ((1, 4),), [(wide * chan, LANES)]
        )
        last = slot(info, [narrowing], sums4)
        g1, stats10 = in_vmem(
            functools.partial(back_merge_kernel, chan),
            [info, *dz4_all, *fars(w4t), far(g2), far(z3), far(zs), norms3, tabs],
            [f32s(rows, wide), f32s(batch, 4 * blocks, LANES)],
            [f32s(rows, wide)],
            after=[last],
        )
        got10 = exchange_batch(stats10)
        last = slot(info, [early, narrowing], dz4_far)
        dz3, dzs, *sent, stats11, sums3 = in_vmem(
            functools.partial(back_enlarge_kernel, batch, chan),
            [
                far(first_enlarge_kernel), info, got10, g1, far(z3), far(zs), norms3, tabs, counts,
                *fars(near2), norms2,
            ],
            [(*full, "far"), (*full, "far"), *shares, routed, f32s(4 * blocks, LANES)],
            [f32s(rows, mid)],
            after=[last],
        )
        got11 = exchange(stats11)
        parts = deliver(sent)
        widening = Gradient(
            wide_products,
            [a2, dz3, even, dzs],
            [(mid, wide), (depth, wide)],
            ((1, 1), (1, 2)),
            [(mid, wide), (depth, wide)],
        )
        last = slot(info, [widening, early, narrowing], dz3)
        dz2, moved2, sums2 = in_vmem(
            back_strided_kernel,
            [info, got11, *parts, far(near2[0]), norms2, tabs, counts],
            [piece, ((rows, 4 * LANES), BF, "far"), f32s(8, LANES)],
            [((2, rows + CHUNK, LANES), BF)],
            after=[last],
        )
        dz2_all = gather_direct(dz2)
        last = slot(info, [widening, early, narrowing], moved2)
        u1, stats12 = in_vmem(
            functools.partial(back_first_kernel, chan),
            [info, *dz2_all, *fars(w2t), far(z1), norms1, tabs],
            [f32s(large, LANES), f32s(batch, 8, LANES)],
            [((2, rows + CHUNK, mid), BF), ((3, 3, LANES, mid), BF), f32s(2, rows, LANES)],
            after=[last],
        )
        got12 = exchange_batch(stats12)
        strided = Gradient(
            strided_products, [a1, moved2], [(mid, tap_lanes)], ((9, 1),), [(9, mid, LANES)]
        )
        last = slot(info, [strided, widening], moved2)
        dz1, sums1, dz1_far = in_vmem(
            back_first_own_kernel,
            [info, got12, u1, far(z1), norms1, tabs, counts],
            [line, f32s(8, LANES), (*line, "far")],
            after=[last],
        )
        dz1_all = gather(dz1)
        dzs_all = gather(dzs)
        reducing = Gradient(
            rows_products, [*source_far, dz1_far], [(depth, LANES)], ((1, 2),), [(depth, LANES)]
        )
        last = slot(info, [reducing, strided, widening], dz1_far)
        (inputs_grad,) = in_vmem(
            functools.partial(leave_kernel, chan),
            [info, *dz1_all, *fars(dzs_all), *fars(w1t), *fars(wpt)],
            [((side, side, images, quarter), BF, "far")],
            [f32s(large, quarter), f32s(rows, quarter)],
            after=[last],
        )
        last = slot(info, [strided, reducing, early, narrowing], inputs_grad)
        everything = [strided, widening, reducing, early, narrowing]
        while any(g.result is None for g in everything):
            last = slot(info, [g for g in everything if g.result is None], last)
        (expanding_grad, middle_grad), (narrowing_grad,) = early.result, narrowing.result
        (widening_grad, shortcut_grad), (spatial_grad,), (reducing_grad,) = (
            g.result for g in (widening, strided, reducing)
        )
        tapped = (3, 3, mid, LANES)
        gains3, gains_s, shift3 = (sums3[n * blocks : (n + 1) * blocks].reshape(-1) for n in range(3))
        gains6, shift6 = sums6[:blocks].reshape(-1), sums6[blocks:].reshape(-1)
        return (
            result.transpose(2, 0, 1, 3),
            inputs_grad.transpose(2, 0, 1, 3),
            reducing_grad,
            spatial_grad.reshape(tapped),
            widening_grad,
            shortcut_grad,
            narrowing_grad,
            middle_grad.reshape(tapped),
            expanding_grad,
            jnp.stack([sums1[0], sums2[0], sums4[0], sums5[0]]),
            jnp.stack([sums1[1], sums2[1], sums4[1], sums5[1]]),
            jnp.stack([gains3, gains_s, gains6]),
            jnp.stack([shift3, shift3, shift6]),
        )

    wide_act = P("batch", None, None, "chan")
    cols = P(None, "chan")
    taps = P(None, None, None, "chan")
    return jax.shard_map(
        local,
        mesh=mesh,
        in_specs=(wide_act, P("batch", None), wide_act, cols, taps, cols, cols, cols, taps)
        + (cols,) * 5,
        out_specs=(wide_act, wide_act, cols, taps, cols, cols, cols, taps) + (cols,) * 5,
        check_vma=False,
    )
```

time: 541 us -> 446 us (0.82)
  waiting for transfers between devices: 283 us -> 161 us
  starting transfers between devices: 83.1 us -> 148 us
  Pallas kernels: 89.3 us -> 125 us
  local copies, waits for them, and re-layouts: 29 us -> 6.99 us
  matrix products: 21.1 us -> 0 us
  other arithmetic: 18.3 us -> 1.31 us
  between operations: 15.1 us -> 1.53 us
    psum x1 -> x0, waiting for transfers between devices: 125 us -> none  [local(): grads = [lax.psum(v.astype(BF), 'batch').astype(F32) for v in grads]]
    ppermute x57 -> x84, starting transfers between devices: 36.5 us -> 88.1 us  [swap(): lax.ppermute(v, axis, [(k, k ^ mask) for k in range(mesh.shape[axis])])]
    pallas_call x19 -> x31, Pallas kernels: 89.3 us -> 125 us  [in_vmem(): pl.pallas_call(body, out_shape=shapes, in_specs=specs, out_specs=out_spec...]
    ppermute x57 -> x84, waiting for transfers between devices: 114 us -> 141 us  [swap(): lax.ppermute(v, axis, [(k, k ^ mask) for k in range(mesh.shape[axis])])]
    unnamed x189 -> x52, local copies, waits for them, and re-layouts: 22.8 us -> 1.25 us
    dot_general x18 -> x0, matrix products: 21.1 us -> none  [dot(): return lax.dot_general(a, b, (dims, ((), ())), preferred_element_type=F32)]
    all_to_all x4, waiting for transfers between devices: 22.5 us -> 4.68 us  [exchange_batch(): return lax.all_to_all(stats, 'batch', 0, 0)]
    convert_element_type x7 -> x0, other arithmetic: 10.2 us -> none  [local(): grads = [lax.psum(v.astype(BF), 'batch').astype(F32) for v in grads]]
  transfers between devices with their start and end apart: 70 -> 96, of which waited for: 31 -> 40; matrix products, arithmetic and copies ran while one was open for 6% -> 1% of each run, Pallas kernels for 7% -> 18%
where the time goes in v1:
time: 446 us; the launch traced here: 444 us
  waiting for transfers between devices  161 us (36%)
  starting transfers between devices  148 us (33%)
  Pallas kernels  125 us (28%)
  local copies, waits for them, and re-layouts  6.99 us (2%)
    ppermute x84, waiting for transfers between devices, swap(): lax.ppermute(v, axis, [(k, k ^ mask) for k in range(mesh.shape[axis])])  141 us
    pallas_call x31, Pallas kernels, in_vmem(): pl.pallas_call(body, out_shape=shapes, in_specs=specs, out_specs=out_spec...  125 us
    ppermute x84, starting transfers between devices, swap(): lax.ppermute(v, axis, [(k, k ^ mask) for k in range(mesh.shape[axis])])  88.1 us
    all_to_all x8, starting transfers between devices, exchange(): return lax.all_to_all(stats, everyone, 0, 0)  40.5 us
    all_to_all x4, starting transfers between devices, exchange_batch(): return lax.all_to_all(stats, 'batch', 0, 0)  18.9 us
    all_to_all x8, waiting for transfers between devices, exchange(): return lax.all_to_all(stats, everyone, 0, 0)  15.5 us
  transfers between devices with their start and end apart: 96, of which 40 were waited for; matrix products, arithmetic and copies ran while one was open for 1% of the time, Pallas kernels for 18%

profile of v1, /device:TPU:0, one launch (start us, length us, event | category | flops | bytes accessed | tf_op | source)
XLA Modules:
  0.0 443.8 jit_solution(8157032646697650390)
XLA Ops:
  6.4 17.9 %collective-permute-done.1.refs_4_ = bf16[1568,256]{1,0:T(8,128)(2,1)S(1)} collective-permute-done((bf16[1568,256]{1,0:T(8,128)(2,1)S(1)}, bf16[1568,256]{1,0:T(8,128)(2,1)S(1)}, u32[]{:S(2)}, u32[]{:S(2)}) %collective-permute-start.1) | collective-permute-done | bytes 802848 | tf_op jit(solution)/shard_map/ppermute | solution.py:1064
  74.3 5.1 %all-to-all-start.2 = ((f32[32,8,128]{2,1,0:T(8,128)}), f32[32,8,128]{2,1,0:T(8,128)S(1)}, u32[]{:S(2)}, u32[]{:S(2)}) async-start(f32[32,8,128]{2,1,0:T(8,128)} %get-tuple-element.171), calls=%async_computation.2 | async-start | bytes 262144 | tf_op jit(solution)/shard_map/all_to_all | solution.py:1085
  79.6 11.8 %all-to-all-done.2.refs_1_ = f32[32,8,128]{2,1,0:T(8,128)S(1)} async-done(((f32[32,8,128]{2,1,0:T(8,128)}), f32[32,8,128]{2,1,0:T(8,128)S(1)}, u32[]{:S(2)}, u32[]{:S(2)}) %all-to-all-start.2) | async-done | bytes 131104 | tf_op jit(solution)/shard_map/all_to_all | solution.py:1085
  138.5 5.0 %all-to-all-start.5 = ((f32[8,8,128]{2,1,0:T(8,128)}), f32[8,8,128]{2,1,0:T(8,128)S(1)}, u32[]{:S(2)}, u32[]{:S(2)}) async-start(f32[8,8,128]{2,1,0:T(8,128)} %get-tuple-element.180), calls=%async_computation.5 | async-start | bytes 65536 | tf_op jit(solution)/shard_map/all_to_all | solution.py:1088
  170.3 5.8 %all-to-all-start.7 = ((f32[32,8,128]{2,1,0:T(8,128)}), f32[32,8,128]{2,1,0:T(8,128)S(1)}, u32[]{:S(2)}, u32[]{:S(2)}) async-start(f32[32,8,128]{2,1,0:T(8,128)} %get-tuple-element.193), calls=%async_computation.7 | async-start | bytes 262144 | tf_op jit(solution)/shard_map/all_to_all | solution.py:1085
  178.2 5.2 %collective-permute-done.35.refs_9_ = bf16[448,128]{1,0:T(8,128)(2,1)S(1)} collective-permute-done((bf16[448,128]{1,0:T(8,128)(2,1)S(1)}, bf16[448,128]{1,0:T(8,128)(2,1)S(1)}, u32[]{:S(2)}, u32[]{:S(2)}) %collective-permute-start.35) | collective-permute-done | bytes 114720 | tf_op jit(solution)/shard_map/ppermute | solution.py:1064
  185.0 6.0 %shard_map.249 = (bf16[448,1152]{1,0:T(8,128)(2,1)}, f32[448,128]{1,0:T(8,128)S(1)}, bf16[448,128]{1,0:T(8,128)(2,1)S(1)}, bf16[448,128]{1,0:T(8,128)(2,1)S(1)},...) custom-call(bf16[256,512]{1,0:T(8,128)(2,1)} %get-tuple-element.317.refs_0_.refs_14_, ...), custom_call_target="tpu_custom_call" | custom-call | flops 4000000000 | tf_op jit(solution)/shard_map/pallas_call | solution.py:234
  191.1 5.0 %all-to-all-start.8 = ((f32[32,8,128]{2,1,0:T(8,128)}), f32[32,8,128]{2,1,0:T(8,128)S(1)}, u32[]{:S(2)}, u32[]{:S(2)}) async-start(f32[32,8,128]{2,1,0:T(8,128)} %get-tuple-element.209), calls=%async_computation.8 | async-start | bytes 262144 | tf_op jit(solution)/shard_map/all_to_all | solution.py:1085
  220.1 5.5 %all-to-all-start.9 = ((f32[8,16,128]{2,1,0:T(8,128)}), f32[8,16,128]{2,1,0:T(8,128)S(1)}, u32[]{:S(2)}, u32[]{:S(2)}) async-start(f32[8,16,128]{2,1,0:T(8,128)} %get-tuple-element.228), calls=%async_computation.9 | async-start | bytes 131072 | tf_op jit(solution)/shard_map/all_to_all | solution.py:1088
  237.5 5.7 %shard_map.255 = (bf16[448,512]{1,0:T(8,128)(2,1)}, bf16[448,512]{1,0:T(8,128)(2,1)}, f32[448,128]{1,0:T(8,128)S(1)}, bf16[448,128]{1,0:T(8,128)(2,1)S(1)}, bf16...) custom-call(bf16[13,64,128]{2,1,0:T(8,128)(2,1)} %get-tuple-element.223., ...), custom_call_target="tpu_custom_call" | custom-call | flops 4000000000 | tf_op jit(solution)/shard_map/pallas_call | solution.py:234
  246.4 11.2 %collective-permute-done.46.refs_8_ = bf16[17,64,128]{2,1,0:T(8,128)(2,1)S(1)} collective-permute-done((bf16[17,64,128]{2,1,0:T(8,128)(2,1)}, bf16[17,64,128]{2,1,0:T(8,128)(2,1)S(1)}, u32[]{:S(2)}, u32[]{:S(2)}) %collective-permute-start.46) | collective-permute-done | bytes 278560 | tf_op jit(solution)/shard_map/ppermute | solution.py:1064
  257.6 5.0 %shard_map.256 = (bf16[48,64,128]{2,1,0:T(8,128)(2,1)}, bf16[13,64,128]{2,1,0:T(8,128)(2,1)}, bf16[4,64,128]{2,1,0:T(8,128)(2,1)}, bf16[48,64,128]{2,1,0:T(8,128...) custom-call(bf16[448,512]{1,0:T(8,128)(2,1)} %get-tuple-element.235.refs_0_.refs_3_, ...), custom_call_target="tpu_custom_call" | custom-call | flops 4000000000 | tf_op jit(solution)/shard_map/pallas_call | solution.py:234
  264.2 7.1 %all-to-all-start.10 = ((f32[32,8,128]{2,1,0:T(8,128)}), f32[32,8,128]{2,1,0:T(8,128)S(1)}, u32[]{:S(2)}, u32[]{:S(2)}) async-start(f32[32,8,128]{2,1,0:T(8,128)} %get-tuple-element.244), calls=%async_computation.10 | async-start | bytes 262144 | tf_op jit(solution)/shard_map/all_to_all | solution.py:1085
  288.7 8.9 %collective-permute-done.53.refs_6_ = bf16[17,64,128]{2,1,0:T(8,128)(2,1)S(1)} collective-permute-done((bf16[17,64,128]{2,1,0:T(8,128)(2,1)}, bf16[17,64,128]{2,1,0:T(8,128)(2,1)S(1)}, u32[]{:S(2)}, u32[]{:S(2)}) %collective-permute-start.53) | collective-permute-done | bytes 278560 | tf_op jit(solution)/shard_map/ppermute | solution.py:1064
  301.5 5.8 %collective-permute-start.55 = (bf16[12,64,128]{2,1,0:T(8,128)(2,1)}, bf16[12,64,128]{2,1,0:T(8,128)(2,1)S(1)}, u32[]{:S(2)}, u32[]{:S(2)}) collective-permute-start(bf16[12,64,128]{2,1,0:T(8,128)(2,1)} %get-tuple-element.258), channel_id=1, source_target_pairs={{0,8},{4,12},{8,0},{12,4},{16,24},{20,28},{24,16},{28,20},{1,9},{5... | collective-permute-start | bytes 589832 | tf_op jit(solution)/shard_map/ppermute | solution.py:1064
  314.8 9.9 %collective-permute-done.56.refs_6_ = bf16[12,64,128]{2,1,0:T(8,128)(2,1)S(1)} collective-permute-done((bf16[12,64,128]{2,1,0:T(8,128)(2,1)}, bf16[12,64,128]{2,1,0:T(8,128)(2,1)S(1)}, u32[]{:S(2)}, u32[]{:S(2)}) %collective-permute-start.56) | collective-permute-done | bytes 196640 | tf_op jit(solution)/shard_map/ppermute | solution.py:1064
  324.7 5.4 %shard_map.259 = (bf16[36,64,128]{2,1,0:T(8,128)(2,1)}, bf16[12,64,128]{2,1,0:T(8,128)(2,1)}, bf16[36,64,128]{2,1,0:T(8,128)(2,1)}, bf16[12,64,128]{2,1,0:T(8,12...) custom-call(bf16[448,512]{1,0:T(8,128)(2,1)} %get-tuple-element.249.refs_0_.refs_3_, ...), custom_call_target="tpu_custom_call" | custom-call | flops 4000000000 | tf_op jit(solution)/shard_map/pallas_call | solution.py:234
  331.7 5.4 %shard_map.260 = (f32[1568,128]{1,0:T(8,128)S(1)}, f32[8,8,128]{2,1,0:T(8,128)}) custom-call(bf16[12,64,128]{2,1,0:T(8,128)(2,1)} %get-tuple-element.257.refs_4_.refs_0_, s32[18]{0:T(128)S(1)} %pad_add_fusion.refs_0_.refs_1_.refs_13_.refs_5_.refs_2_, bf16[448,128]{1,0:T(8,128)(2,1)S(1)} %get-tuple-element.262.refs_2_, ...), custom_call_target="tpu_custom_call" | custom-call | flops 4000000000 | tf_op jit(solution)/shard_map/pallas_call | solution.py:234
  337.1 5.0 %all-to-all-start.11 = ((f32[8,8,128]{2,1,0:T(8,128)}), f32[8,8,128]{2,1,0:T(8,128)S(1)}, u32[]{:S(2)}, u32[]{:S(2)}) async-start(f32[8,8,128]{2,1,0:T(8,128)} %get-tuple-element.265), calls=%async_computation.11 | async-start | bytes 65536 | tf_op jit(solution)/shard_map/all_to_all | solution.py:1088
  351.9 9.4 %collective-permute-done.63.refs_11_ = bf16[12,64,128]{2,1,0:T(8,128)(2,1)S(1)} collective-permute-done((bf16[12,64,128]{2,1,0:T(8,128)(2,1)S(1)}, bf16[12,64,128]{2,1,0:T(8,128)(2,1)S(1)}, u32[]{:S(2)}, u32[]{:S(2)}) %collective-permute-start.63) | collective-permute-done | bytes 196640 | tf_op jit(solution)/shard_map/ppermute | solution.py:1064
  363.3 5.5 %shard_map.262 = (bf16[8,64,128]{2,1,0:T(8,128)(2,1)}, bf16[9,64,128]{2,1,0:T(8,128)(2,1)}, bf16[48,64,128]{2,1,0:T(8,128)(2,1)}, bf16[56,64,128]{2,1,0:T(8,128)...) custom-call(bf16[1568,128]{1,0:T(8,128)(2,1)} %get-tuple-element.267.refs_0_.refs_6_, ...), custom_call_target="tpu_custom_call" | custom-call | flops 4000000000 | tf_op jit(solution)/shard_map/pallas_call | solution.py:234
  376.4 6.8 %shard_map.263.refs_0_ = bf16[14,14,8,256]{3,2,1,0:T(8,128)(2,1)} custom-call(bf16[8,64,128]{2,1,0:T(8,128)(2,1)} %get-tuple-element.277.refs_0_.refs_6_, s32[18]{0:T(128)S(1)} %pad_add_fusion.refs_0_.refs_1_.refs_13_.refs_5_.refs_2_, bf16[1568,128]{1,0:T(8,128)(2,1)S(1)} %get-tuple-element.278.refs_2_, ...), custom_call_target="tpu_custom_call" | custom-call | flops 4000000000 | tf_op jit(solution)/shard_map/pallas_call | solution.py:234
  388.7 9.8 %collective-permute-done.74.refs_7_ = bf16[56,64,128]{2,1,0:T(8,128)(2,1)S(1)} collective-permute-done((bf16[56,64,128]{2,1,0:T(8,128)(2,1)}, bf16[56,64,128]{2,1,0:T(8,128)(2,1)S(1)}, u32[]{:S(2)}, u32[]{:S(2)}) %collective-permute-start.74) | collective-permute-done | bytes 917536 | tf_op jit(solution)/shard_map/ppermute | solution.py:1064
  410.4 5.9 %collective-permute-done.77.refs_4_ = bf16[11,64,128]{2,1,0:T(8,128)(2,1)S(1)} collective-permute-done((bf16[11,64,128]{2,1,0:T(8,128)(2,1)}, bf16[11,64,128]{2,1,0:T(8,128)(2,1)S(1)}, u32[]{:S(2)}, u32[]{:S(2)}) %collective-permute-start.77) | collective-permute-done | bytes 180256 | tf_op jit(solution)/shard_map/ppermute | solution.py:1064
  (270 shorter events, 267.8 us)
Async XLA Ops:
  3.4 20.9 %collective-permute-start.1 = (bf16[1568,256]{1,0:T(8,128)(2,1)S(1)}, bf16[1568,256]{1,0:T(8,128)(2,1)S(1)}, u32[]{:S(2)}, u32[]{:S(2)}) collective-permute-start(bf16[1568,256]{1,0:T(8,128)(2,1)S(1)} %shard_map.237.refs_2_), channel_id=1, source_target_pairs={{0,2},{1,3},{2,0},{3,1},{4,6},{5,7},{6,4},{7,5},{8,10},{9,11},{10,... | collective-permute-start | bytes 2408456 | tf_op jit(solution)/shard_map/ppermute | solution.py:1064
  6.4 20.2 %collective-permute-start = (bf16[1568,256]{1,0:T(8,128)(2,1)S(1)}, bf16[1568,256]{1,0:T(8,128)(2,1)S(1)}, u32[]{:S(2)}, u32[]{:S(2)}) collective-permute-start(bf16[1568,256]{1,0:T(8,128)(2,1)S(1)} %shard_map.237.refs_2_), channel_id=1, source_target_pairs={{0,1},{1,0},{2,3},{3,2},{4,5},{5,4},{6,7},{7,6},{8,9},{9,8},{10,11... | collective-permute-start | bytes 2408456 | tf_op jit(solution)/shard_map/ppermute | solution.py:1064
  60.7 18.9 %collective-permute-start.13 = (bf16[448,512]{1,0:T(8,128)(2,1)S(1)}, bf16[448,512]{1,0:T(8,128)(2,1)S(1)}, u32[]{:S(2)}, u32[]{:S(2)}) collective-permute-start(bf16[448,512]{1,0:T(8,128)(2,1)S(1)} %copy-done.13), channel_id=1, source_target_pairs={{0,2},{1,3},{2,0},{3,1},{4,6},{5,7},{6,4},{7,5},{8,10},{9,11},{10,... | collective-permute-start | bytes 1376264 | tf_op jit(solution)/shard_map/ppermute | solution.py:1064
  73.4 18.0 %collective-permute-start.12 = (bf16[448,512]{1,0:T(8,128)(2,1)S(1)}, bf16[448,512]{1,0:T(8,128)(2,1)S(1)}, u32[]{:S(2)}, u32[]{:S(2)}) collective-permute-start(bf16[448,512]{1,0:T(8,128)(2,1)S(1)} %get-tuple-element.173.refs_3_), channel_id=1, source_target_pairs={{0,2},{1,3},{2,0},{3,1},{4,6},{5,7},{6,4},{7,5},{8,10},{9,11},{10,... | collective-permute-start | bytes 1376264 | tf_op jit(solution)/shard_map/ppermute | solution.py:1064
  123.8 21.3 %collective-permute-start.30 = (bf16[256,128]{1,0:T(8,128)(2,1)}, bf16[256,128]{1,0:T(8,128)(2,1)}, u32[]{:S(2)}, u32[]{:S(2)}) collective-permute-start(bf16[256,128]{1,0:T(8,128)(2,1)} %get-tuple-element.323), channel_id=1, source_target_pairs={{0,3},{1,2},{2,1},{3,0},{4,7},{5,6},{6,5},{7,4},{8,11},{9,10},{10,... | collective-permute-start | bytes 196616 | tf_op jit(solution)/shard_map/ppermute | solution.py:1064
  125.4 19.9 %collective-permute-start.28 = (bf16[256,128]{1,0:T(8,128)(2,1)}, bf16[256,128]{1,0:T(8,128)(2,1)}, u32[]{:S(2)}, u32[]{:S(2)}) collective-permute-start(bf16[256,128]{1,0:T(8,128)(2,1)} %get-tuple-element.324), channel_id=1, source_target_pairs={{0,1},{1,0},{2,3},{3,2},{4,5},{5,4},{6,7},{7,6},{8,9},{9,8},{10,11... | collective-permute-start | bytes 196616 | tf_op jit(solution)/shard_map/ppermute | solution.py:1064
  131.7 26.6 %collective-permute-start.29 = (bf16[256,128]{1,0:T(8,128)(2,1)S(1)}, bf16[256,128]{1,0:T(8,128)(2,1)}, u32[]{:S(2)}, u32[]{:S(2)}) collective-permute-start(bf16[256,128]{1,0:T(8,128)(2,1)S(1)} %get-tuple-element.326), channel_id=1, source_target_pairs={{0,2},{1,3},{2,0},{3,1},{4,6},{5,7},{6,4},{7,5},{8,10},{9,11},{10,... | collective-permute-start | bytes 196616 | tf_op jit(solution)/shard_map/ppermute | solution.py:1064
  134.4 24.0 %collective-permute-start.33 = (bf16[512,128]{1,0:T(8,128)(2,1)}, bf16[512,128]{1,0:T(8,128)(2,1)}, u32[]{:S(2)}, u32[]{:S(2)}) collective-permute-start(bf16[512,128]{1,0:T(8,128)(2,1)} %get-tuple-element.319), channel_id=1, source_target_pairs={{0,3},{1,2},{2,1},{3,0},{4,7},{5,6},{6,5},{7,4},{8,11},{9,10},{10,... | collective-permute-start | bytes 393224 | tf_op jit(solution)/shard_map/ppermute | solution.py:1064
  144.4 20.3 %collective-permute-start.27 = (bf16[3,3,128,128]{3,2,1,0:T(8,128)(2,1)}, bf16[3,3,128,128]{3,2,1,0:T(8,128)(2,1)}, u32[]{:S(2)}, u32[]{:S(2)}) collective-permute-start(bf16[3,3,128,128]{3,2,1,0:T(8,128)(2,1)} %get-tuple-element.311), channel_id=1, source_target_pairs={{0,3},{1,2},{2,1},{3,0},{4,7},{5,6},{6,5},{7,4},{8,11},{9,10},{10,... | collective-permute-start | bytes 884744 | tf_op jit(solution)/shard_map/ppermute | solution.py:1064
  145.2 20.3 %collective-permute-start.25 = (bf16[3,3,128,128]{3,2,1,0:T(8,128)(2,1)}, bf16[3,3,128,128]{3,2,1,0:T(8,128)(2,1)}, u32[]{:S(2)}, u32[]{:S(2)}) collective-permute-start(bf16[3,3,128,128]{3,2,1,0:T(8,128)(2,1)} %get-tuple-element.312), channel_id=1, source_target_pairs={{0,1},{1,0},{2,3},{3,2},{4,5},{5,4},{6,7},{7,6},{8,9},{9,8},{10,11... | collective-permute-start | bytes 884744 | tf_op jit(solution)/shard_map/ppermute | solution.py:1064
  145.3 20.1 %collective-permute-start.26 = (bf16[3,3,128,128]{3,2,1,0:T(8,128)(2,1)S(1)}, bf16[3,3,128,128]{3,2,1,0:T(8,128)(2,1)}, u32[]{:S(2)}, u32[]{:S(2)}) collective-permute-start(bf16[3,3,128,128]{3,2,1,0:T(8,128)(2,1)S(1)} %get-tuple-element.314), channel_id=1, source_target_pairs={{0,2},{1,3},{2,0},{3,1},{4,6},{5,7},{6,4},{7,5},{8,10},{9,11},{10,... | collective-permute-start | bytes 884744 | tf_op jit(solution)/shard_map/ppermute | solution.py:1064
  160.2 18.0 %collective-permute-start.24 = (bf16[256,512]{1,0:T(8,128)(2,1)}, bf16[256,512]{1,0:T(8,128)(2,1)S(1)}, u32[]{:S(2)}, u32[]{:S(2)}) collective-permute-start(bf16[256,512]{1,0:T(8,128)(2,1)} %get-tuple-element.315), channel_id=1, source_target_pairs={{0,3},{1,2},{2,1},{3,0},{4,7},{5,6},{6,5},{7,4},{8,11},{9,10},{10,... | collective-permute-start | bytes 786440 | tf_op jit(solution)/shard_map/ppermute | solution.py:1064
  202.7 27.4 %collective-permute-start.40 = (bf16[52,64,128]{2,1,0:T(8,128)(2,1)}, bf16[52,64,128]{2,1,0:T(8,128)(2,1)S(1)}, u32[]{:S(2)}, u32[]{:S(2)}) collective-permute-start(bf16[52,64,128]{2,1,0:T(8,128)(2,1)} %get-tuple-element.215), channel_id=1, source_target_pairs={{0,4},{4,0},{8,12},{12,8},{16,20},{20,16},{24,28},{28,24},{1,5},{5... | collective-permute-start | bytes 2555912 | tf_op jit(solution)/shard_map/ppermute | solution.py:1064
  235.0 22.6 %collective-permute-start.46 = (bf16[17,64,128]{2,1,0:T(8,128)(2,1)}, bf16[17,64,128]{2,1,0:T(8,128)(2,1)S(1)}, u32[]{:S(2)}, u32[]{:S(2)}) collective-permute-start(bf16[17,64,128]{2,1,0:T(8,128)(2,1)} %get-tuple-element.240), channel_id=1, source_target_pairs={{0,16},{4,20},{8,24},{12,28},{16,0},{20,4},{24,8},{28,12},{1,17},{... | collective-permute-start | bytes 835592 | tf_op jit(solution)/shard_map/ppermute | solution.py:1064
  237.5 20.1 %collective-permute-start.47 = (bf16[17,64,128]{2,1,0:T(8,128)(2,1)}, bf16[17,64,128]{2,1,0:T(8,128)(2,1)S(1)}, u32[]{:S(2)}, u32[]{:S(2)}) collective-permute-start(bf16[17,64,128]{2,1,0:T(8,128)(2,1)} %get-tuple-element.241), channel_id=1, source_target_pairs={{0,24},{4,28},{8,16},{12,20},{16,8},{20,12},{24,0},{28,4},{1,25},{... | collective-permute-start | bytes 835592 | tf_op jit(solution)/shard_map/ppermute | solution.py:1064
  262.6 35.0 %collective-permute-start.51 = (bf16[48,64,128]{2,1,0:T(8,128)(2,1)}, bf16[48,64,128]{2,1,0:T(8,128)(2,1)S(1)}, u32[]{:S(2)}, u32[]{:S(2)}) collective-permute-start(bf16[48,64,128]{2,1,0:T(8,128)(2,1)} %get-tuple-element.251), channel_id=1, source_target_pairs={{0,4},{4,0},{8,12},{12,8},{16,20},{20,16},{24,28},{28,24},{1,5},{5... | collective-permute-start | bytes 2359304 | tf_op jit(solution)/shard_map/ppermute | solution.py:1064
  275.1 22.6 %collective-permute-start.53 = (bf16[17,64,128]{2,1,0:T(8,128)(2,1)}, bf16[17,64,128]{2,1,0:T(8,128)(2,1)S(1)}, u32[]{:S(2)}, u32[]{:S(2)}) collective-permute-start(bf16[17,64,128]{2,1,0:T(8,128)(2,1)} %get-tuple-element.254), channel_id=1, source_target_pairs={{0,16},{4,20},{8,24},{12,28},{16,0},{20,4},{24,8},{28,12},{1,17},{... | collective-permute-start | bytes 835592 | tf_op jit(solution)/shard_map/ppermute | solution.py:1064
  278.6 19.0 %collective-permute-start.54 = (bf16[17,64,128]{2,1,0:T(8,128)(2,1)}, bf16[17,64,128]{2,1,0:T(8,128)(2,1)S(1)}, u32[]{:S(2)}, u32[]{:S(2)}) collective-permute-start(bf16[17,64,128]{2,1,0:T(8,128)(2,1)} %get-tuple-element.255), channel_id=1, source_target_pairs={{0,24},{4,28},{8,16},{12,20},{16,8},{20,12},{24,0},{28,4},{1,25},{... | collective-permute-start | bytes 835592 | tf_op jit(solution)/shard_map/ppermute | solution.py:1064
  309.8 21.9 %collective-permute-start.60 = (bf16[448,128]{1,0:T(8,128)(2,1)S(1)}, bf16[448,128]{1,0:T(8,128)(2,1)S(1)}, u32[]{:S(2)}, u32[]{:S(2)}) collective-permute-start(bf16[448,128]{1,0:T(8,128)(2,1)S(1)} %get-tuple-element.262.refs_2_), channel_id=1, source_target_pairs={{0,3},{1,2},{2,1},{3,0},{4,7},{5,6},{6,5},{7,4},{8,11},{9,10},{10,... | collective-permute-start | bytes 344072 | tf_op jit(solution)/shard_map/ppermute | solution.py:1064
  309.8 21.9 %collective-permute-start.59 = (bf16[448,128]{1,0:T(8,128)(2,1)S(1)}, bf16[448,128]{1,0:T(8,128)(2,1)S(1)}, u32[]{:S(2)}, u32[]{:S(2)}) collective-permute-start(bf16[448,128]{1,0:T(8,128)(2,1)S(1)} %get-tuple-element.262.refs_2_), channel_id=1, source_target_pairs={{0,2},{1,3},{2,0},{3,1},{4,6},{5,7},{6,4},{7,5},{8,10},{9,11},{10,... | collective-permute-start | bytes 344072 | tf_op jit(solution)/shard_map/ppermute | solution.py:1064
  330.1 33.2 %collective-permute-start.61 = (bf16[36,64,128]{2,1,0:T(8,128)(2,1)}, bf16[36,64,128]{2,1,0:T(8,128)(2,1)S(1)}, u32[]{:S(2)}, u32[]{:S(2)}) collective-permute-start(bf16[36,64,128]{2,1,0:T(8,128)(2,1)} %get-tuple-element.272), channel_id=1, source_target_pairs={{0,4},{4,0},{8,12},{12,8},{16,20},{20,16},{24,28},{28,24},{1,5},{5... | collective-permute-start | bytes 1769480 | tf_op jit(solution)/shard_map/ppermute | solution.py:1064
  342.2 27.3 %collective-permute-start.69 = (bf16[448,512]{1,0:T(8,128)(2,1)S(1)}, bf16[448,512]{1,0:T(8,128)(2,1)S(1)}, u32[]{:S(2)}, u32[]{:S(2)}) collective-permute-start(bf16[448,512]{1,0:T(8,128)(2,1)S(1)} %copy-done.14), channel_id=1, source_target_pairs={{0,2},{1,3},{2,0},{3,1},{4,6},{5,7},{6,4},{7,5},{8,10},{9,11},{10,... | collective-permute-start | bytes 1376264 | tf_op jit(solution)/shard_map/ppermute | solution.py:1064
  361.3 27.4 %collective-permute-start.75 = (bf16[68,64,128]{2,1,0:T(8,128)(2,1)S(1)}, bf16[68,64,128]{2,1,0:T(8,128)(2,1)S(1)}, u32[]{:S(2)}, u32[]{:S(2)}) collective-permute-start(bf16[68,64,128]{2,1,0:T(8,128)(2,1)S(1)} %copy-done.12), channel_id=1, source_target_pairs={{0,4},{4,0},{8,12},{12,8},{16,20},{20,16},{24,28},{28,24},{1,5},{5... | collective-permute-start | bytes 3342344 | tf_op jit(solution)/shard_map/ppermute | solution.py:1064
  368.9 29.7 %collective-permute-start.74 = (bf16[56,64,128]{2,1,0:T(8,128)(2,1)}, bf16[56,64,128]{2,1,0:T(8,128)(2,1)S(1)}, u32[]{:S(2)}, u32[]{:S(2)}) collective-permute-start(bf16[56,64,128]{2,1,0:T(8,128)(2,1)} %get-tuple-element.283), channel_id=1, source_target_pairs={{0,4},{4,0},{8,12},{12,8},{16,20},{20,16},{24,28},{28,24},{1,5},{5... | collective-permute-start | bytes 2752520 | tf_op jit(solution)/shard_map/ppermute | solution.py:1064
  (98 other events, 955.9 us)
